TPU v7x, 32 devices: a whole 2x2x4 slice. The times are simulated.
32 devices in a mesh: dp: 4 (over y, x), tensor: 8 (over z, core).
Axes of the slice: x: 2, y: 2, z: 4, core: 2. Of those that a mesh axis runs over, the one named last changes fastest.
Arguments:
- grad_out: bfloat16 [2048, 8192], P('dp', 'tensor'), may hold values from -6 to 6
- down_weight: bfloat16 [8192, 24576], P(None, 'tensor'), may hold values from -0.0625 to 0.0625
- quantized: bfloat16 [2048, 24576], P('dp', 'tensor'), may hold values from -0.125 to 0.125
- clip_mask: int32 [2048, 24576], P('dp', 'tensor'), may hold values 0 or 1
- first_rot: bfloat16 [192, 128, 128], P('tensor'), may hold values from -0.5 to 0.5
- second_rot: bfloat16 [192, 128, 128], P('tensor'), may hold values from -0.5 to 0.5
- block_order: int32 [192], replicated, may hold values from 0 to 191, each once
Outputs:
- grad_hidden: bfloat16 [2048, 24576], P('dp', 'tensor')
- grad_weight: bfloat16 [8192, 24576], P('dp', 'tensor')
Inputs may be any that keep to these rules, and one draw needn't show every extreme that they name: `block_order`: a permutation of the blocks.
All inputs are finite; a program needn't handle non-finite values. No bound on the sum of `clip_mask` on one device may be relied on, other than what follows from the above.
Results may differ from a plain program's by a relative error of at most 0.009.
Values may be sent and summed in bfloat16 or wider, within the bound.
No kernel may reach another device: no remote copies, remote signals or barrier semaphores. Data moves between devices by JAX's collectives and lax.ppermute only.
A program may use at most 320 MiB of HBM per device.

v0:
```python
import functools

import jax
import jax.numpy as jnp
from jax import lax
from jax.experimental import pallas as pl
from jax.experimental.pallas import tpu as pltpu
from jax.sharding import PartitionSpec as P

CHUNKS = 2
VMEM_LIMIT = 56 * 1024 * 1024
ANY = pl.BlockSpec(memory_space=pl.ANY)


def rows_at(index, count):
    return pl.ds(pl.multiple_of(index * count, count), count)


def params(limit=VMEM_LIMIT):
    return pltpu.CompilerParams(vmem_limit_bytes=limit)


def cost(flops, nbytes):
    return pl.CostEstimate(flops=int(flops), bytes_accessed=int(nbytes), transcendentals=0)


def project_kernel(devices, groups, tile, chunk, place_ref, *refs):
    given = len(refs) - groups - 7
    bufs, (w_ref, mask_ref, rot_ref, out_ref) = refs[:given], refs[given : given + 4]
    shards, (dy, sems, shard_sems) = refs[given + 4 : -3], refs[-3:]
    me, group = place_ref[0], place_ref[1]
    rows, width = dy.shape[0], dy.shape[1] // devices

    def gather(action):
        for x in range(devices):
            if len(bufs) == 1:
                source, shard = bufs[0].at[x], x
            else:
                source, shard = bufs[x], me ^ x
            if source.shape[0] != rows:
                source = source.at[chunk * rows : (chunk + 1) * rows]
            action(pltpu.make_async_copy(source, dy.at[:, rows_at(shard, width)], sems.at[x]))

    def share(action):
        for m, shard in enumerate(shards):
            source = dy.at[:, rows_at(2 * (group ^ m) + me % 2, width)]
            action(pltpu.make_async_copy(source, shard, shard_sems.at[m]))

    @pl.when(pl.program_id(0) == 0)
    def _():
        gather(lambda copy: copy.start())
        gather(lambda copy: copy.wait())
        share(lambda copy: copy.start())

    product = jnp.dot(dy[...], w_ref[...], preferred_element_type=jnp.float32)
    masked = (product * mask_ref[...].astype(jnp.float32)).astype(jnp.bfloat16)
    block = rot_ref.shape[1]
    for b in range(tile // block):
        turned = lax.dot_general(
            masked[:, b * block : (b + 1) * block],
            rot_ref[b],
            (((1,), (1,)), ((), ())),
            preferred_element_type=jnp.float32,
        )
        out_ref[:, b * block : (b + 1) * block] = turned.astype(jnp.bfloat16)

    @pl.when(pl.program_id(0) == pl.num_programs(0) - 1)
    def _():
        share(lambda copy: copy.wait())


def project(place, bufs, weight, mask, rot, chunk, groups, tile_blocks=4):
    rows, width = bufs[-1].shape[-2:]
    depth, units = weight.shape
    devices = depth // width
    block = rot.shape[1]
    tile = tile_blocks * block
    permuted, *shards = pl.pallas_call(
        functools.partial(project_kernel, devices, groups, tile, chunk),
        grid_spec=pltpu.PrefetchScalarGridSpec(
            num_scalar_prefetch=1,
            grid=(units // tile,),
            in_specs=[ANY] * len(bufs)
            + [
                pl.BlockSpec((depth, tile), lambda j, _: (0, j)),
                pl.BlockSpec((rows, tile), lambda j, _: (chunk, j)),
                pl.BlockSpec((tile // block, block, block), lambda j, _: (j, 0, 0)),
            ],
            out_specs=[pl.BlockSpec((rows, tile), lambda j, _: (0, j))] + [ANY] * groups,
            scratch_shapes=[
                pltpu.VMEM((rows, depth), jnp.bfloat16),
                pltpu.SemaphoreType.DMA((devices,)),
                pltpu.SemaphoreType.DMA((groups,)),
            ],
        ),
        out_shape=[jax.ShapeDtypeStruct((rows, units), jnp.bfloat16)]
        + [jax.ShapeDtypeStruct((rows, width), jnp.bfloat16)] * groups,
        compiler_params=params(),
        cost_estimate=cost(2 * rows * depth * units, 2 * depth * units + 2 * rows * depth + 8 * rows * units),
    )(place, *bufs, weight, mask, rot)
    return permuted, shards


def reorder_kernel(block, order_ref, in_ref, out_ref):
    per = in_ref.shape[2] // block
    for source in range(in_ref.shape[0]):
        for b in range(per):
            to = order_ref[source * per + b]
            out_ref[to // per, :, rows_at(to % per, block)] = in_ref[source, :, b * block : (b + 1) * block]


def reorder(order, pieces, block):
    devices, rows, units = pieces.shape
    step = min(rows, 16)
    spec = pl.BlockSpec((devices, step, units), lambda i, _: (0, i, 0))
    return pl.pallas_call(
        functools.partial(reorder_kernel, block),
        grid_spec=pltpu.PrefetchScalarGridSpec(
            num_scalar_prefetch=1, grid=(rows // step,), in_specs=[spec], out_specs=spec
        ),
        out_shape=jax.ShapeDtypeStruct(pieces.shape, jnp.bfloat16),
        compiler_params=params(),
        cost_estimate=cost(0, 4 * devices * rows * units),
    )(order, pieces)


def rotate_kernel(piece_ref, rot_ref, *refs):
    out_ref = refs[-1]
    block = rot_ref.shape[1]
    for b in range(rot_ref.shape[0]):
        turned = lax.dot_general(
            piece_ref[:, b * block : (b + 1) * block],
            rot_ref[b],
            (((1,), (1,)), ((), ())),
            preferred_element_type=jnp.float32,
        )
        out_ref[:, b * block : (b + 1) * block] = turned.astype(jnp.bfloat16)


def rotate(piece, rot, chunk, chunks, so_far):
    rows, units = piece.shape
    block = rot.shape[1]
    tile = 8 * block
    held = [] if so_far is None else [so_far]
    return pl.pallas_call(
        rotate_kernel,
        grid=(units // tile,),
        in_specs=[
            pl.BlockSpec((rows, tile), lambda j: (0, j)),
            pl.BlockSpec((tile // block, block, block), lambda j: (j, 0, 0)),
        ]
        + [ANY] * len(held),
        out_specs=pl.BlockSpec((rows, tile), lambda j: (chunk, j)),
        out_shape=jax.ShapeDtypeStruct((rows * chunks, units), jnp.bfloat16),
        input_output_aliases={2: 0} if held else {},
        compiler_params=params(),
        cost_estimate=cost(2 * rows * units * block, 4 * rows * units),
    )(piece, rot, *held)


def weight_kernel(count, place_ref, *refs):
    pieces, values, (out_ref, turned) = refs[:count], refs[count:-2], refs[-2:]
    rows = pieces[0].shape[0]

    @pl.when(pl.program_id(0) == 0)
    def _():
        for n, piece in enumerate(pieces):
            turned[:, n * rows : (n + 1) * rows] = piece[...].T

    total, at = None, 0
    for value in values:
        tokens = value.shape[0]
        part = jnp.dot(turned[:, at : at + tokens], value[...], preferred_element_type=jnp.float32)
        total = part if total is None else total + part
        at += tokens
    out_ref[...] = total.astype(jnp.bfloat16)


def weight_kernel_held(count, place_ref, *refs):
    weight_kernel(count, place_ref, *refs[:-3], *refs[-2:])


def weight_rows(core, pieces, values, so_far, tile=512):
    rows, width = pieces[0].shape
    units = values[0].shape[1]
    total = rows * len(pieces)
    held = [] if so_far is None else [so_far]
    return pl.pallas_call(
        functools.partial(weight_kernel_held if held else weight_kernel, len(pieces)),
        grid_spec=pltpu.PrefetchScalarGridSpec(
            num_scalar_prefetch=1,
            grid=(units // tile,),
            in_specs=[pl.BlockSpec((rows, width), lambda j, _: (0, 0))] * len(pieces)
            + [pl.BlockSpec((value.shape[0], tile), lambda j, _: (0, j)) for value in values]
            + [ANY] * len(held),
            out_specs=pl.BlockSpec((width, tile), lambda j, core: (core[0], j)),
            scratch_shapes=[pltpu.VMEM((width, total), jnp.bfloat16)],
        ),
        out_shape=jax.ShapeDtypeStruct((2 * width, units), jnp.bfloat16),
        input_output_aliases={1 + len(pieces) + len(values): 0} if held else {},
        compiler_params=params(),
        cost_estimate=cost(2 * width * total * units, 2 * width * total + 2 * total * units + 2 * width * units),
    )(core, *pieces, *values, *held)


def after(values, *others):
    return lax.optimization_barrier((values, *others))[0]


def swap(values, axis, bits):
    size = lax.axis_size(axis)
    return lax.ppermute(values, axis, [(t, t ^ bits) for t in range(size)])


def exchange(values, axis):
    return lax.all_to_all(values, axis, split_axis=0, concat_axis=0, tiled=True)


def per_device(grad_out, down_weight, quantized, clip_mask, first_rot, second_rot, block_order):
    devices, groups = lax.axis_size("tensor"), lax.axis_size("dp")
    me, group = lax.axis_index("tensor"), lax.axis_index("dp")
    place = jnp.stack([me, group]).astype(jnp.int32)
    core = (me % 2).astype(jnp.int32)[None]
    block = first_rot.shape[1]
    units = quantized.shape[1]
    tokens = grad_out.shape[0]
    rows = tokens // CHUNKS
    top, low = quantized[: tokens // 2], quantized[tokens // 2 :]
    weights = down_weight, clip_mask, second_rot

    full0 = lax.all_gather(grad_out[:rows], "tensor", axis=0)
    x_top, y_top = swap(top, "dp", 1), swap(top, "dp", 2)
    full1 = lax.all_gather(grad_out[rows:], "tensor", axis=0)
    low_now = after(low, x_top, y_top)
    x_low, y_low = swap(low_now, "dp", 1), swap(low_now, "dp", 2)
    permuted, shards = project(place, [after(full0, x_top, y_top)], *weights, 0, groups)
    sent = exchange(permuted.reshape(devices, rows // devices, units), "tensor")
    first = [shard if m == 0 else swap(shard, "dp", m) for m, shard in enumerate(shards)]
    xy_top, xy_low = swap(x_top, "dp", 2), swap(y_low, "dp", 1)
    permuted, shards = project(place, [after(full1, permuted, x_low, y_low)], *weights, 1, groups)
    permuted = after(permuted, xy_top, xy_low)
    placed = reorder(block_order, after(sent, permuted, *first), block)
    sent = exchange(permuted.reshape(devices, rows // devices, units), "tensor")
    second = [shard if m == 0 else swap(after(shard, permuted, *first), "dp", m) for m, shard in enumerate(shards)]
    mine = [piece for pair in zip(first, second) for piece in pair]
    returned = exchange(after(placed, sent), "tensor").reshape(rows, units)
    placed = reorder(block_order, after(sent, placed, *mine), block)
    theirs = [swap(value, "tensor", 1) for value in mine]
    values = [quantized, x_top, x_low, y_top, y_low, xy_top, xy_low]
    grad_weight = weight_rows(core, mine, [quantized, *values[1:-1], after(xy_low, placed)], None)
    last = exchange(after(placed, returned, grad_weight), "tensor").reshape(rows, units)
    grad_weight = weight_rows(1 - core, theirs, values, grad_weight)
    grad_hidden = rotate(returned, first_rot, 0, CHUNKS, None)
    grad_hidden = rotate(last, first_rot, 1, CHUNKS, grad_hidden)
    return (grad_hidden, grad_weight)


def block_apply(values, rotations):
    count, width = rotations.shape[:2]
    shaped = values.reshape(values.shape[0], count, width)
    result = jnp.einsum("tbi,bji->tbj", shaped, rotations, preferred_element_type=jnp.float32)
    return result.reshape(values.shape[0], count * width).astype(jnp.bfloat16)


def per_device_wide(grad_out, down_weight, quantized, clip_mask, first_rot, second_rot, block_order):
    tokens, units = quantized.shape
    devices = lax.axis_size("tensor")
    gathered = lax.all_gather(quantized, "dp", axis=0, tiled=True)
    full = lax.all_gather(grad_out, "tensor", axis=1, tiled=True)
    rows = lax.all_to_all(full, "dp", split_axis=1, concat_axis=0, tiled=True)
    grad_weight = lax.dot_general(
        rows, gathered, (((0,), (0,)), ((), ())), preferred_element_type=jnp.float32
    ).astype(jnp.bfloat16)
    product = jnp.dot(full, down_weight, preferred_element_type=jnp.float32)
    permuted = block_apply((product * clip_mask).astype(jnp.bfloat16), second_rot)
    blocks, width = block_order.shape[0], first_rot.shape[1]
    inverse = jnp.zeros((blocks,), jnp.int32).at[block_order].set(jnp.arange(blocks, dtype=jnp.int32))
    received = lax.all_to_all(
        permuted.reshape(devices, tokens // devices, units), "tensor", split_axis=0, concat_axis=2, tiled=True
    )
    lead, items = received.shape[:2]
    placed = jnp.take(received.reshape(lead, items, blocks, width), inverse, axis=2)
    returned = lax.all_to_all(
        placed.reshape(lead, items, blocks * width), "tensor", split_axis=2, concat_axis=0, tiled=True
    )
    grad_hidden = block_apply(returned.reshape(tokens, units), first_rot)
    return (grad_hidden, grad_weight)


def solution(mesh):
    placed = (
        P("dp", "tensor"),
        P(None, "tensor"),
        P("dp", "tensor"),
        P("dp", "tensor"),
        P("tensor", None, None),
        P("tensor", None, None),
        P(),
    )
    short = mesh.shape["tensor"] == 8 and mesh.shape["dp"] == 4
    return jax.shard_map(
        per_device if short else per_device_wide,
        mesh=mesh,
        in_specs=placed,
        out_specs=(P("dp", "tensor"), P("dp", "tensor")),
        check_vma=False,
    )
```

profile of v0, /device:TPU:0, one launch (start us, length us, event | category | flops | bytes accessed | tf_op | source)
XLA Modules:
  0.0 304.8 jit_solution(8150747144546913908)
XLA Ops:
  7.2 2.4 fusion.1
  10.4 1.9 fusion
  12.3 2.9 collective-permute-start
  15.2 1.5 collective-permute-start.1
  17.4 32.4 %collective-permute-done.refs_9_ = bf16[256,3072]{1,0:T(8,128)(2,1)S(1)} collective-permute-done((bf16[256,3072]{1,0:T(8,128)(2,1)}, bf16[256,3072]{1,0:T(8,128)(2,1)S(1)}, u32[]{:S(2)}, u32[]{:S(2)}) %collective-permute-start) | collective-permute-done | bytes 1572896 | tf_op jit(solution)/shard_map/ppermute | solution.py:212
  51.6 1.7 collective-permute-start.3
  53.4 6.3 %all-gather.7.cloned.1.call-done = bf16[2048,1024]{1,0:T(8,128)(2,1)} async-done(((bf16[256,1024]{1,0:T(8,128)(2,1)}), bf16[2048,1024]{1,0:T(8,128)(2,1)}) %all-gather.7.cloned.1.call-update) | async-done | bytes 4194320 | tf_op jit(solution)/shard_map/all_gather | solution.py:231
  59.7 28.0 %shard_map.86 = (bf16[256,3072]{1,0:T(8,128)(2,1)}, bf16[256,1024]{1,0:T(8,128)(2,1)}, bf16[256,1024]{1,0:T(8,128)(2,1)}, bf16[256,1024]{1,0:T(8,128)(2,1)}, bf16[256,1024]{1,0:T(8,128)(2,1)}) custom-call(s32[2]{0:T(128)} %pad_add_fusion.place_ref, bf16[8,256,1024]{2,1,0:T(8,128)(2,1)} %bitcast.12, bf16[8192,3072]{1,0:T(8,128)(2,1)} %refs_1_.3, ...), custom_call_target="tpu_custom_call" | custom-call | flops 12884901888 | bytes 60817408 | tf_op jit(solution)/shard_map/pallas_call | solution.py:78
  87.7 3.6 %all-to-all-start.1 = ((bf16[8,32,3072]{2,1,0:T(8,128)(2,1)}), bf16[8,32,3072]{2,1,0:T(8,128)(2,1)S(1)}, u32[]{:S(2)}, u32[]{:S(2)}) async-start(bf16[8,32,3072]{2,1,0:T(8,128)(2,1)} %bitcast.14), calls=%async_computation.1 | async-start | bytes 3145728 | tf_op jit(solution)/shard_map/all_to_all | solution.py:216
  91.3 1.5 collective-permute-start.4
  92.8 1.5 collective-permute-start.5
  94.2 23.8 %all-gather.5.cloned.1.call-done = bf16[2048,1024]{1,0:T(8,128)(2,1)} async-done(((bf16[256,1024]{1,0:T(8,128)(2,1)}), bf16[2048,1024]{1,0:T(8,128)(2,1)}) %all-gather.5.cloned.1.call-update) | async-done | bytes 4194320 | tf_op jit(solution)/shard_map/all_gather | solution.py:233
  118.0 27.5 %shard_map.87 = (bf16[256,3072]{1,0:T(8,128)(2,1)}, bf16[256,1024]{1,0:T(8,128)(2,1)}, bf16[256,1024]{1,0:T(8,128)(2,1)}, bf16[256,1024]{1,0:T(8,128)(2,1)}, bf16[256,1024]{1,0:T(8,128)(2,1)}) custom-call(s32[2]{0:T(128)} %pad_add_fusion.place_ref, bf16[8,256,1024]{2,1,0:T(8,128)(2,1)} %bitcast.11, bf16[8192,3072]{1,0:T(8,128)(2,1)} %refs_1_.3, ...), custom_call_target="tpu_custom_call" | custom-call | flops 12884901888 | bytes 60817408 | tf_op jit(solution)/shard_map/pallas_call | solution.py:78
  146.7 6.8 %all-to-all-start = ((bf16[8,32,3072]{2,1,0:T(8,128)(2,1)}), bf16[8,32,3072]{2,1,0:T(8,128)(2,1)S(1)}, u32[]{:S(2)}, u32[]{:S(2)}) async-start(bf16[8,32,3072]{2,1,0:T(8,128)(2,1)} %bitcast.13), calls=%async_computation | async-start | bytes 3145728 | tf_op jit(solution)/shard_map/all_to_all | solution.py:216
  153.5 2.0 collective-permute-start.6
  155.5 1.5 collective-permute-start.7
  157.0 11.6 %collective-permute-done.6.refs_2_ = bf16[256,1024]{1,0:T(8,128)(2,1)} collective-permute-done((bf16[256,1024]{1,0:T(8,128)(2,1)}, bf16[256,1024]{1,0:T(8,128)(2,1)}, u32[]{:S(2)}, u32[]{:S(2)}) %collective-permute-start.6) | collective-permute-done | bytes 524320 | tf_op jit(solution)/shard_map/ppermute | solution.py:212
  168.6 12.5 %collective-permute-done.7.refs_4_ = bf16[256,1024]{1,0:T(8,128)(2,1)} collective-permute-done((bf16[256,1024]{1,0:T(8,128)(2,1)}, bf16[256,1024]{1,0:T(8,128)(2,1)}, u32[]{:S(2)}, u32[]{:S(2)}) %collective-permute-start.7) | collective-permute-done | bytes 524320 | tf_op jit(solution)/shard_map/ppermute | solution.py:212
  181.1 6.0 %shard_map.88 = bf16[8,32,3072]{2,1,0:T(8,128)(2,1)} custom-call(s32[192]{0:T(256)} %order_ref.3, bf16[8,32,3072]{2,1,0:T(8,128)(2,1)} %copy-done.1), custom_call_target="tpu_custom_call" | custom-call | bytes 3145728 | tf_op jit(solution)/shard_map/pallas_call | solution.py:116
  187.1 4.3 %all-to-all-done.in_ref = bf16[8,32,3072]{2,1,0:T(8,128)(2,1)S(1)} async-done(((bf16[8,32,3072]{2,1,0:T(8,128)(2,1)}), bf16[8,32,3072]{2,1,0:T(8,128)(2,1)S(1)}, u32[]{:S(2)}, u32[]{:S(2)}) %all-to-all-start) | async-done | bytes 1572896 | tf_op jit(solution)/shard_map/all_to_all | solution.py:216
  192.5 3.6 %all-to-all-start.2 = ((bf16[8,32,3072]{2,1,0:T(8,128)(2,1)}), bf16[8,32,3072]{2,1,0:T(8,128)(2,1)S(1)}, u32[]{:S(2)}, u32[]{:S(2)}) async-start(bf16[8,32,3072]{2,1,0:T(8,128)(2,1)} %shard_map.88), calls=%async_computation.2 | async-start | bytes 3145728 | tf_op jit(solution)/shard_map/all_to_all | solution.py:216
  196.1 2.0 collective-permute-start.9
  198.1 1.5 collective-permute-start.10
  199.6 11.4 %collective-permute-done.9.refs_3_ = bf16[256,1024]{1,0:T(8,128)(2,1)S(1)} collective-permute-done((bf16[256,1024]{1,0:T(8,128)(2,1)}, bf16[256,1024]{1,0:T(8,128)(2,1)S(1)}, u32[]{:S(2)}, u32[]{:S(2)}) %collective-permute-start.9) | collective-permute-done | bytes 524320 | tf_op jit(solution)/shard_map/ppermute | solution.py:212
  211.0 12.4 %collective-permute-done.10.refs_5_ = bf16[256,1024]{1,0:T(8,128)(2,1)S(1)} collective-permute-done((bf16[256,1024]{1,0:T(8,128)(2,1)}, bf16[256,1024]{1,0:T(8,128)(2,1)S(1)}, u32[]{:S(2)}, u32[]{:S(2)}) %collective-permute-start.10) | collective-permute-done | bytes 524320 | tf_op jit(solution)/shard_map/ppermute | solution.py:212
  223.4 6.0 %shard_map.89 = bf16[8,32,3072]{2,1,0:T(8,128)(2,1)} custom-call(s32[192]{0:T(256)} %order_ref.3, bf16[8,32,3072]{2,1,0:T(8,128)(2,1)} %copy-done), custom_call_target="tpu_custom_call" | custom-call | bytes 3145728 | tf_op jit(solution)/shard_map/pallas_call | solution.py:116
  229.5 19.6 %shard_map.90.refs_15_ = bf16[2048,3072]{1,0:T(8,128)(2,1)} custom-call(s32[1]{0:T(128)} %bitcast.7.place_ref, bf16[256,1024]{1,0:T(8,128)(2,1)} %get-tuple-element.30.refs_0_, bf16[256,1024]{1,0:T(8,128)(2,1)} %get-tuple-element.35.refs_1_, bf16[256,1024]{1,0:T(8,128)(2,1)} %collective-permute-done.6.refs_2_, bf16[256,1024]{1,0:T(8,128)(2,1)} %copy-done.7, ...), custom_call_target="tpu_custom_call" | custom-call | flops 12884901888 | bytes 23068672 | tf_op jit(solution)/shard_map/pallas_call | solution.py:188
  250.2 4.8 %all-to-all-start.3 = ((bf16[8,32,3072]{2,1,0:T(8,128)(2,1)}), bf16[8,32,3072]{2,1,0:T(8,128)(2,1)S(1)}, u32[]{:S(2)}, u32[]{:S(2)}) async-start(bf16[8,32,3072]{2,1,0:T(8,128)(2,1)} %shard_map.89), calls=%async_computation.3 | async-start | bytes 3145728 | tf_op jit(solution)/shard_map/all_to_all | solution.py:216
  259.1 4.0 %shard_map.91.refs_0_ = bf16[512,3072]{1,0:T(8,128)(2,1)} custom-call(bf16[256,3072]{1,0:T(8,128)(2,1)} %bitcast.9, bf16[24,128,128]{2,1,0:T(8,128)(2,1)} %rot_ref.3), custom_call_target="tpu_custom_call" | custom-call | flops 201326592 | bytes 3145728 | tf_op jit(solution)/shard_map/pallas_call | solution.py:145
  265.2 19.5 %shard_map.93 = bf16[2048,3072]{1,0:T(8,128)(2,1)} custom-call(s32[1]{0:T(128)S(6)} %sub.3.place_ref, bf16[256,1024]{1,0:T(8,128)(2,1)} %copy-done.10, bf16[256,1024]{1,0:T(8,128)(2,1)} %copy-done.11, bf16[256,1024]{1,0:T(8,128)(2,1)} %copy-done.12, bf16[256,1024]{1,0:T(8,128)(2,1)} %copy-done.15, ...), custom_call_target="tpu_custom_call", output_to_operand_aliasing={{}: (16, {})} | custom-call | flops 12884901888 | bytes 23068672 | tf_op jit(solution)/shard_map/pallas_call | solution.py:188
  284.8 8.0 %all-to-all-done.3 = bf16[8,32,3072]{2,1,0:T(8,128)(2,1)S(1)} async-done(((bf16[8,32,3072]{2,1,0:T(8,128)(2,1)}), bf16[8,32,3072]{2,1,0:T(8,128)(2,1)S(1)}, u32[]{:S(2)}, u32[]{:S(2)}) %all-to-all-start.3) | async-done | bytes 1572896 | tf_op jit(solution)/shard_map/all_to_all | solution.py:216
  294.0 4.0 %shard_map.92 = bf16[512,3072]{1,0:T(8,128)(2,1)} custom-call(bf16[256,3072]{1,0:T(8,128)(2,1)} %bitcast.10, bf16[24,128,128]{2,1,0:T(8,128)(2,1)} %rot_ref.3, bf16[512,3072]{1,0:T(8,128)(2,1)} %shard_map.91.refs_0_), custom_call_target="tpu_custom_call", output_to_operand_aliasing={{}: (2, {})} | custom-call | flops 201326592 | bytes 3145728 | tf_op jit(solution)/shard_map/pallas_call | solution.py:145
  (69 shorter events, 14.2 us)
Async XLA Ops:
  7.2 52.5 %all-gather.7.cloned.1.call-start = ((), (), s32[]{:S(2)}) async-start(), calls=%async_computation.5 | async-start | bytes 4718592 | tf_op jit(solution)/shard_map/all_gather | solution.py:231
  9.7 108.4 %all-gather.5.cloned.1.call-start = ((), (), s32[]{:S(2)}) async-start(), calls=%async_computation.4 | async-start | bytes 4718592 | tf_op jit(solution)/shard_map/all_gather | solution.py:233
  12.3 37.5 %collective-permute-start = (bf16[256,3072]{1,0:T(8,128)(2,1)}, bf16[256,3072]{1,0:T(8,128)(2,1)S(1)}, u32[]{:S(2)}, u32[]{:S(2)}) collective-permute-start(bf16[256,3072]{1,0:T(8,128)(2,1)} %get-tuple-element.47), channel_id=1, source_target_pairs={{0,8},{8,0},{16,24},{24,16},{1,9},{9,1},{17,25},{25,17},{2,10},{10... | collective-permute-start | bytes 4718600 | tf_op jit(solution)/shard_map/ppermute | solution.py:212
  15.2 36.1 %collective-permute-start.1 = (bf16[256,3072]{1,0:T(8,128)(2,1)}, bf16[256,3072]{1,0:T(8,128)(2,1)S(1)}, u32[]{:S(2)}, u32[]{:S(2)}) collective-permute-start(bf16[256,3072]{1,0:T(8,128)(2,1)} %get-tuple-element.47), channel_id=1, source_target_pairs={{0,16},{8,24},{16,0},{24,8},{1,17},{9,25},{17,1},{25,9},{2,18},{10... | collective-permute-start | bytes 4718600 | tf_op jit(solution)/shard_map/ppermute | solution.py:212
  49.8 41.4 %copy-start.5 = (bf16[256,3072]{1,0:T(8,128)(2,1)}, bf16[256,3072]{1,0:T(8,128)(2,1)S(1)}, u32[]{:S(2)}) copy-start(bf16[256,3072]{1,0:T(8,128)(2,1)S(1)} %collective-permute-done.refs_9_) | copy-start | bytes 4718596
  51.3 36.4 %copy-start.6 = (bf16[256,3072]{1,0:T(8,128)(2,1)}, bf16[256,3072]{1,0:T(8,128)(2,1)S(1)}, u32[]{:S(2)}) copy-start(bf16[256,3072]{1,0:T(8,128)(2,1)S(1)} %collective-permute-done.1.refs_11_) | copy-start | bytes 4718596
  51.3 42.9 %collective-permute-start.2 = (bf16[256,3072]{1,0:T(8,128)(2,1)}, bf16[256,3072]{1,0:T(8,128)(2,1)}, u32[]{:S(2)}, u32[]{:S(2)}) collective-permute-start(bf16[256,3072]{1,0:T(8,128)(2,1)} %get-tuple-element.26), channel_id=1, source_target_pairs={{0,8},{8,0},{16,24},{24,16},{1,9},{9,1},{17,25},{25,17},{2,10},{10... | collective-permute-start | bytes 4718600 | tf_op jit(solution)/shard_map/ppermute | solution.py:212
  51.6 41.1 %collective-permute-start.3 = (bf16[256,3072]{1,0:T(8,128)(2,1)}, bf16[256,3072]{1,0:T(8,128)(2,1)}, u32[]{:S(2)}, u32[]{:S(2)}) collective-permute-start(bf16[256,3072]{1,0:T(8,128)(2,1)} %get-tuple-element.26), channel_id=1, source_target_pairs={{0,16},{8,24},{16,0},{24,8},{1,17},{9,25},{17,1},{25,9},{2,18},{10... | collective-permute-start | bytes 4718600 | tf_op jit(solution)/shard_map/ppermute | solution.py:212
  87.7 57.9 %all-to-all-start.1 = ((bf16[8,32,3072]{2,1,0:T(8,128)(2,1)}), bf16[8,32,3072]{2,1,0:T(8,128)(2,1)S(1)}, u32[]{:S(2)}, u32[]{:S(2)}) async-start(bf16[8,32,3072]{2,1,0:T(8,128)(2,1)} %bitcast.14), calls=%async_computation.1 | async-start | bytes 3145728 | tf_op jit(solution)/shard_map/all_to_all | solution.py:216
  91.3 54.2 %collective-permute-start.4 = (bf16[256,3072]{1,0:T(8,128)(2,1)S(1)}, bf16[256,3072]{1,0:T(8,128)(2,1)}, u32[]{:S(2)}, u32[]{:S(2)}) collective-permute-start(bf16[256,3072]{1,0:T(8,128)(2,1)S(1)} %collective-permute-done.refs_9_), channel_id=1, source_target_pairs={{0,16},{8,24},{16,0},{24,8},{1,17},{9,25},{17,1},{25,9},{2,18},{10... | collective-permute-start | bytes 4718600 | tf_op jit(solution)/shard_map/ppermute | solution.py:212
  92.8 52.8 %collective-permute-start.5 = (bf16[256,3072]{1,0:T(8,128)(2,1)}, bf16[256,3072]{1,0:T(8,128)(2,1)}, u32[]{:S(2)}, u32[]{:S(2)}) collective-permute-start(bf16[256,3072]{1,0:T(8,128)(2,1)} %collective-permute-done.3.refs_12_), channel_id=1, source_target_pairs={{0,8},{8,0},{16,24},{24,16},{1,9},{9,1},{17,25},{25,17},{2,10},{10... | collective-permute-start | bytes 4718600 | tf_op jit(solution)/shard_map/ppermute | solution.py:212
  146.7 44.6 %all-to-all-start = ((bf16[8,32,3072]{2,1,0:T(8,128)(2,1)}), bf16[8,32,3072]{2,1,0:T(8,128)(2,1)S(1)}, u32[]{:S(2)}, u32[]{:S(2)}) async-start(bf16[8,32,3072]{2,1,0:T(8,128)(2,1)} %bitcast.13), calls=%async_computation | async-start | bytes 3145728 | tf_op jit(solution)/shard_map/all_to_all | solution.py:216
  153.5 15.1 %collective-permute-start.6 = (bf16[256,1024]{1,0:T(8,128)(2,1)}, bf16[256,1024]{1,0:T(8,128)(2,1)}, u32[]{:S(2)}, u32[]{:S(2)}) collective-permute-start(bf16[256,1024]{1,0:T(8,128)(2,1)} %get-tuple-element.31), channel_id=1, source_target_pairs={{0,8},{8,0},{16,24},{24,16},{1,9},{9,1},{17,25},{25,17},{2,10},{10... | collective-permute-start | bytes 1572872 | tf_op jit(solution)/shard_map/ppermute | solution.py:212
  155.5 25.6 %collective-permute-start.7 = (bf16[256,1024]{1,0:T(8,128)(2,1)}, bf16[256,1024]{1,0:T(8,128)(2,1)}, u32[]{:S(2)}, u32[]{:S(2)}) collective-permute-start(bf16[256,1024]{1,0:T(8,128)(2,1)} %get-tuple-element.32), channel_id=1, source_target_pairs={{0,16},{8,24},{16,0},{24,8},{1,17},{9,25},{17,1},{25,9},{2,18},{10... | collective-permute-start | bytes 1572872 | tf_op jit(solution)/shard_map/ppermute | solution.py:212
  156.9 24.1 %collective-permute-start.8 = (bf16[256,1024]{1,0:T(8,128)(2,1)}, bf16[256,1024]{1,0:T(8,128)(2,1)}, u32[]{:S(2)}, u32[]{:S(2)}) collective-permute-start(bf16[256,1024]{1,0:T(8,128)(2,1)} %get-tuple-element.33), channel_id=1, source_target_pairs={{0,24},{8,16},{16,8},{24,0},{1,25},{9,17},{17,9},{25,1},{2,26},{10... | collective-permute-start | bytes 1572872 | tf_op jit(solution)/shard_map/ppermute | solution.py:212
  192.5 56.6 %all-to-all-start.2 = ((bf16[8,32,3072]{2,1,0:T(8,128)(2,1)}), bf16[8,32,3072]{2,1,0:T(8,128)(2,1)S(1)}, u32[]{:S(2)}, u32[]{:S(2)}) async-start(bf16[8,32,3072]{2,1,0:T(8,128)(2,1)} %shard_map.88), calls=%async_computation.2 | async-start | bytes 3145728 | tf_op jit(solution)/shard_map/all_to_all | solution.py:216
  196.1 15.0 %collective-permute-start.9 = (bf16[256,1024]{1,0:T(8,128)(2,1)}, bf16[256,1024]{1,0:T(8,128)(2,1)S(1)}, u32[]{:S(2)}, u32[]{:S(2)}) collective-permute-start(bf16[256,1024]{1,0:T(8,128)(2,1)} %get-tuple-element.37), channel_id=1, source_target_pairs={{0,8},{8,0},{16,24},{24,16},{1,9},{9,1},{17,25},{25,17},{2,10},{10... | collective-permute-start | bytes 1572872 | tf_op jit(solution)/shard_map/ppermute | solution.py:212
  198.1 25.3 %collective-permute-start.10 = (bf16[256,1024]{1,0:T(8,128)(2,1)}, bf16[256,1024]{1,0:T(8,128)(2,1)S(1)}, u32[]{:S(2)}, u32[]{:S(2)}) collective-permute-start(bf16[256,1024]{1,0:T(8,128)(2,1)} %get-tuple-element.39), channel_id=1, source_target_pairs={{0,16},{8,24},{16,0},{24,8},{1,17},{9,25},{17,1},{25,9},{2,18},{10... | collective-permute-start | bytes 1572872 | tf_op jit(solution)/shard_map/ppermute | solution.py:212
  199.6 23.9 %collective-permute-start.11 = (bf16[256,1024]{1,0:T(8,128)(2,1)}, bf16[256,1024]{1,0:T(8,128)(2,1)S(1)}, u32[]{:S(2)}, u32[]{:S(2)}) collective-permute-start(bf16[256,1024]{1,0:T(8,128)(2,1)} %get-tuple-element.41), channel_id=1, source_target_pairs={{0,24},{8,16},{16,8},{24,0},{1,25},{9,17},{17,9},{25,1},{2,26},{10... | collective-permute-start | bytes 1572872 | tf_op jit(solution)/shard_map/ppermute | solution.py:212
  211.0 18.4 %copy-start.7 = (bf16[256,1024]{1,0:T(8,128)(2,1)}, bf16[256,1024]{1,0:T(8,128)(2,1)S(1)}, u32[]{:S(2)}) copy-start(bf16[256,1024]{1,0:T(8,128)(2,1)S(1)} %collective-permute-done.9.refs_3_) | copy-start | bytes 1572868
  223.4 6.0 %copy-start.8 = (bf16[256,1024]{1,0:T(8,128)(2,1)}, bf16[256,1024]{1,0:T(8,128)(2,1)S(1)}, u32[]{:S(2)}) copy-start(bf16[256,1024]{1,0:T(8,128)(2,1)S(1)} %collective-permute-done.10.refs_5_) | copy-start | bytes 1572868
  223.4 6.0 %copy-start.9 = (bf16[256,1024]{1,0:T(8,128)(2,1)}, bf16[256,1024]{1,0:T(8,128)(2,1)S(1)}, u32[]{:S(2)}) copy-start(bf16[256,1024]{1,0:T(8,128)(2,1)S(1)} %collective-permute-done.11.refs_7_) | copy-start | bytes 1572868
  250.2 42.6 %all-to-all-start.3 = ((bf16[8,32,3072]{2,1,0:T(8,128)(2,1)}), bf16[8,32,3072]{2,1,0:T(8,128)(2,1)S(1)}, u32[]{:S(2)}, u32[]{:S(2)}) async-start(bf16[8,32,3072]{2,1,0:T(8,128)(2,1)} %shard_map.89), calls=%async_computation.3 | async-start | bytes 3145728 | tf_op jit(solution)/shard_map/all_to_all | solution.py:216
  255.0 2.4 collective-permute-start.12
  255.5 2.6 collective-permute-start.13
  255.5 3.4 %collective-permute-start.14 = (bf16[256,1024]{1,0:T(8,128)(2,1)}, bf16[256,1024]{1,0:T(8,128)(2,1)S(1)}, u32[]{:S(2)}, u32[]{:S(2)}) collective-permute-start(bf16[256,1024]{1,0:T(8,128)(2,1)} %collective-permute-done.6.refs_2_), channel_id=1, source_target_pairs={{0,1},{1,0},{2,3},{3,2},{4,5},{5,4},{6,7},{7,6},{8,9},{9,8},{10,11... | collective-permute-start | bytes 1572872 | tf_op jit(solution)/shard_map/ppermute | solution.py:212
  256.0 7.1 %collective-permute-start.16 = (bf16[256,1024]{1,0:T(8,128)(2,1)}, bf16[256,1024]{1,0:T(8,128)(2,1)S(1)}, u32[]{:S(2)}, u32[]{:S(2)}) collective-permute-start(bf16[256,1024]{1,0:T(8,128)(2,1)} %collective-permute-done.7.refs_4_), channel_id=1, source_target_pairs={{0,1},{1,0},{2,3},{3,2},{4,5},{5,4},{6,7},{7,6},{8,9},{9,8},{10,11... | collective-permute-start | bytes 1572872 | tf_op jit(solution)/shard_map/ppermute | solution.py:212
  256.0 7.1 %collective-permute-start.18 = (bf16[256,1024]{1,0:T(8,128)(2,1)}, bf16[256,1024]{1,0:T(8,128)(2,1)S(1)}, u32[]{:S(2)}, u32[]{:S(2)}) collective-permute-start(bf16[256,1024]{1,0:T(8,128)(2,1)} %collective-permute-done.8.refs_6_), channel_id=1, source_target_pairs={{0,1},{1,0},{2,3},{3,2},{4,5},{5,4},{6,7},{7,6},{8,9},{9,8},{10,11... | collective-permute-start | bytes 1572872 | tf_op jit(solution)/shard_map/ppermute | solution.py:212
  257.4 5.7 %copy-start.10 = (bf16[256,1024]{1,0:T(8,128)(2,1)}, bf16[256,1024]{1,0:T(8,128)(2,1)S(1)}, u32[]{:S(2)}) copy-start(bf16[256,1024]{1,0:T(8,128)(2,1)S(1)} %collective-permute-done.12.refs_0_) | copy-start | bytes 1572868
  257.4 5.8 %collective-permute-start.15 = (bf16[256,1024]{1,0:T(8,128)(2,1)}, bf16[256,1024]{1,0:T(8,128)(2,1)S(1)}, u32[]{:S(2)}, u32[]{:S(2)}) collective-permute-start(bf16[256,1024]{1,0:T(8,128)(2,1)} %copy-done.7), channel_id=1, source_target_pairs={{0,1},{1,0},{2,3},{3,2},{4,5},{5,4},{6,7},{7,6},{8,9},{9,8},{10,11... | collective-permute-start | bytes 1572872 | tf_op jit(solution)/shard_map/ppermute | solution.py:212
  258.1 5.1 %collective-permute-start.17 = (bf16[256,1024]{1,0:T(8,128)(2,1)}, bf16[256,1024]{1,0:T(8,128)(2,1)S(1)}, u32[]{:S(2)}, u32[]{:S(2)}) collective-permute-start(bf16[256,1024]{1,0:T(8,128)(2,1)} %copy-done.8), channel_id=1, source_target_pairs={{0,1},{1,0},{2,3},{3,2},{4,5},{5,4},{6,7},{7,6},{8,9},{9,8},{10,11... | collective-permute-start | bytes 1572872 | tf_op jit(solution)/shard_map/ppermute | solution.py:212
  258.9 4.3 %collective-permute-start.19 = (bf16[256,1024]{1,0:T(8,128)(2,1)}, bf16[256,1024]{1,0:T(8,128)(2,1)S(1)}, u32[]{:S(2)}, u32[]{:S(2)}) collective-permute-start(bf16[256,1024]{1,0:T(8,128)(2,1)} %copy-done.9), channel_id=1, source_target_pairs={{0,1},{1,0},{2,3},{3,2},{4,5},{5,4},{6,7},{7,6},{8,9},{9,8},{10,11... | collective-permute-start | bytes 1572872 | tf_op jit(solution)/shard_map/ppermute | solution.py:212
  (12 other events, 22.0 us)
Sparse Core Ops, SparseCore 0:
  9.8 49.8 all-gather.6
  61.3 56.7 all-gather.4
where the time goes:
time: 305 us
  waiting for transfers between devices  127 us (42%)
  Pallas kernels  115 us (38%)
  starting transfers between devices  37.6 us (12%)
  between operations  14.3 us (5%)
  local copies, waits for them, and re-layouts  10.9 us (4%)
    ppermute x20, waiting for transfers between devices, swap(): return lax.ppermute(values, axis, [(t, t ^ bits) for t in range(size)])  83.7 us
    pallas_call x2, Pallas kernels, project(): pl.pallas_call(functools.partial(project_kernel, devices, groups, tile, c...  55.5 us
    pallas_call x2, Pallas kernels, weight_rows(): pl.pallas_call(functools.partial(weight_kernel_held if held else weight_k...  39.1 us
    all_gather x1, waiting for transfers between devices, per_device(): full1 = lax.all_gather(grad_out[rows:], 'tensor', axis=0)  23.8 us
    ppermute x20, starting transfers between devices, swap(): return lax.ppermute(values, axis, [(t, t ^ bits) for t in range(size)])  18.8 us
    all_to_all x4, starting transfers between devices, exchange(): return lax.all_to_all(values, axis, split_axis=0, concat_axis=0, tiled=True)  18.8 us
    all_to_all x4, waiting for transfers between devices, exchange(): return lax.all_to_all(values, axis, split_axis=0, concat_axis=0, tiled=True)  12.3 us
    pallas_call x2, Pallas kernels, reorder(): pl.pallas_call(functools.partial(reorder_kernel, block), grid_spec=pltpu....  12 us
  transfers between devices with their start and end apart: 26, of which 13 were waited for; matrix products, arithmetic and copies ran while one was open for 1% of the time, Pallas kernels for 36%

commit v1 on v0

--- a/solution.py
+++ b/solution.py
@@ -25,21 +25,17 @@
 
 
 def project_kernel(devices, groups, tile, chunk, place_ref, *refs):
-    given = len(refs) - groups - 7
-    bufs, (w_ref, mask_ref, rot_ref, out_ref) = refs[:given], refs[given : given + 4]
-    shards, (dy, sems, shard_sems) = refs[given + 4 : -3], refs[-3:]
+    bufs, (w_ref, mask_ref, rot_ref, out_ref) = refs[:devices], refs[devices : devices + 4]
+    shards, (dy, sems, shard_sems) = refs[devices + 4 : -3], refs[-3:]
     me, group = place_ref[0], place_ref[1]
     rows, width = dy.shape[0], dy.shape[1] // devices
 
     def gather(action):
         for x in range(devices):
-            if len(bufs) == 1:
-                source, shard = bufs[0].at[x], x
-            else:
-                source, shard = bufs[x], me ^ x
+            source = bufs[x]
             if source.shape[0] != rows:
                 source = source.at[chunk * rows : (chunk + 1) * rows]
-            action(pltpu.make_async_copy(source, dy.at[:, rows_at(shard, width)], sems.at[x]))
+            action(pltpu.make_async_copy(source, dy.at[:, rows_at(me ^ x, width)], sems.at[x]))
 
     def share(action):
         for m, shard in enumerate(shards):
@@ -70,9 +66,9 @@
 
 
 def project(place, bufs, weight, mask, rot, chunk, groups, tile_blocks=4):
-    rows, width = bufs[-1].shape[-2:]
+    devices = len(bufs)
+    rows, width = bufs[-1].shape
     depth, units = weight.shape
-    devices = depth // width
     block = rot.shape[1]
     tile = tile_blocks * block
     permuted, *shards = pl.pallas_call(
@@ -158,49 +154,53 @@
     )(piece, rot, *held)
 
 
-def weight_kernel(count, place_ref, *refs):
-    pieces, values, (out_ref, turned) = refs[:count], refs[count:-2], refs[-2:]
+def weight_kernel(add, place_ref, *refs):
+    groups = len(refs) - 4
+    pieces, (q_ref, held_ref, out_ref, turned) = refs[:groups], refs[groups:]
     rows = pieces[0].shape[0]
 
     @pl.when(pl.program_id(0) == 0)
     def _():
-        for n, piece in enumerate(pieces):
-            turned[:, n * rows : (n + 1) * rows] = piece[...].T
-
-    total, at = None, 0
-    for value in values:
-        tokens = value.shape[0]
-        part = jnp.dot(turned[:, at : at + tokens], value[...], preferred_element_type=jnp.float32)
-        total = part if total is None else total + part
-        at += tokens
+        for m, piece in enumerate(pieces):
+            turned[:, rows_at(place_ref[1] ^ m, rows)] = piece[...].T
+
+    values = q_ref[...].reshape(groups * rows, q_ref.shape[-1])
+    total = jnp.dot(turned[...], values, preferred_element_type=jnp.float32)
+    if add:
+        total = total + held_ref[...].astype(jnp.float32)
     out_ref[...] = total.astype(jnp.bfloat16)
 
 
-def weight_kernel_held(count, place_ref, *refs):
-    weight_kernel(count, place_ref, *refs[:-3], *refs[-2:])
-
-
-def weight_rows(core, pieces, values, so_far, tile=512):
+def weight_kernel_first(place_ref, *refs):
+    weight_kernel(False, place_ref, *refs[:-2], None, *refs[-2:])
+
+
+def weight_rows(core, group, pieces, gathered, chunk, held, tile=512):
     rows, width = pieces[0].shape
-    units = values[0].shape[1]
-    total = rows * len(pieces)
-    held = [] if so_far is None else [so_far]
+    groups, _, _, units = gathered.shape
+    total = groups * rows
+    add = chunk > 0
+    out_spec = pl.BlockSpec((width, tile), lambda j, place: (place[0], j))
+    if held is None:
+        kernel, extra = weight_kernel_first, []
+    else:
+        kernel, extra = functools.partial(weight_kernel, add), [out_spec if add else ANY]
     return pl.pallas_call(
-        functools.partial(weight_kernel_held if held else weight_kernel, len(pieces)),
+        kernel,
         grid_spec=pltpu.PrefetchScalarGridSpec(
             num_scalar_prefetch=1,
             grid=(units // tile,),
-            in_specs=[pl.BlockSpec((rows, width), lambda j, _: (0, 0))] * len(pieces)
-            + [pl.BlockSpec((value.shape[0], tile), lambda j, _: (0, j)) for value in values]
-            + [ANY] * len(held),
-            out_specs=pl.BlockSpec((width, tile), lambda j, core: (core[0], j)),
+            in_specs=[pl.BlockSpec((rows, width), lambda j, _: (0, 0))] * groups
+            + [pl.BlockSpec((groups, None, rows, tile), lambda j, _: (0, chunk, 0, j))]
+            + extra,
+            out_specs=out_spec,
             scratch_shapes=[pltpu.VMEM((width, total), jnp.bfloat16)],
         ),
         out_shape=jax.ShapeDtypeStruct((2 * width, units), jnp.bfloat16),
-        input_output_aliases={1 + len(pieces) + len(values): 0} if held else {},
+        input_output_aliases={2 + groups: 0} if extra else {},
         compiler_params=params(),
-        cost_estimate=cost(2 * width * total * units, 2 * width * total + 2 * total * units + 2 * width * units),
-    )(core, *pieces, *values, *held)
+        cost_estimate=cost(2 * width * total * units, 2 * width * total + 2 * total * units + 4 * width * units),
+    )(jnp.stack([core, group]).astype(jnp.int32), *pieces, gathered, *([] if held is None else [held]))
 
 
 def after(values, *others):
@@ -214,42 +214,54 @@
 
 def exchange(values, axis):
     return lax.all_to_all(values, axis, split_axis=0, concat_axis=0, tiled=True)
+
+
+def token_exchange(pieces):
+    return [piece if m == 0 else swap(piece, "dp", m) for m, piece in enumerate(pieces)]
 
 
 def per_device(grad_out, down_weight, quantized, clip_mask, first_rot, second_rot, block_order):
     devices, groups = lax.axis_size("tensor"), lax.axis_size("dp")
     me, group = lax.axis_index("tensor"), lax.axis_index("dp")
     place = jnp.stack([me, group]).astype(jnp.int32)
-    core = (me % 2).astype(jnp.int32)[None]
+    core = me % 2
     block = first_rot.shape[1]
     units = quantized.shape[1]
-    tokens = grad_out.shape[0]
-    rows = tokens // CHUNKS
-    top, low = quantized[: tokens // 2], quantized[tokens // 2 :]
+    rows = grad_out.shape[0] // CHUNKS
     weights = down_weight, clip_mask, second_rot
-
-    full0 = lax.all_gather(grad_out[:rows], "tensor", axis=0)
-    x_top, y_top = swap(top, "dp", 1), swap(top, "dp", 2)
-    full1 = lax.all_gather(grad_out[rows:], "tensor", axis=0)
-    low_now = after(low, x_top, y_top)
-    x_low, y_low = swap(low_now, "dp", 1), swap(low_now, "dp", 2)
-    permuted, shards = project(place, [after(full0, x_top, y_top)], *weights, 0, groups)
+    gathered = lax.all_gather(quantized.reshape(CHUNKS, rows, units), "dp", axis=0)
+
+    own = grad_out[:rows], grad_out[rows:]
+    whole = swap(grad_out, "tensor", 1)
+    far0, near0 = swap(own[0], "tensor", 4), swap(own[0], "tensor", 2)
+    corner0 = swap(after(far0, near0), "tensor", 2)
+    far1 = swap(after(own[1], far0, near0), "tensor", 4)
+    corner1, near1 = swap(far1, "tensor", 2), swap(after(own[1], far1, corner0), "tensor", 2)
+
+    def with_cores(near, far, corner):
+        return [grad_out, whole] + [buf for values in (near, far, corner) for buf in (values, swap(values, "tensor", 1))]
+
+    bufs = with_cores(near0, far0, corner0)
+    bufs[-1] = after(bufs[-1], far1)
+    permuted, shards = project(place, bufs, *weights, 0, groups)
+    permuted = after(permuted, near1, corner1)
     sent = exchange(permuted.reshape(devices, rows // devices, units), "tensor")
-    first = [shard if m == 0 else swap(shard, "dp", m) for m, shard in enumerate(shards)]
-    xy_top, xy_low = swap(x_top, "dp", 2), swap(y_low, "dp", 1)
-    permuted, shards = project(place, [after(full1, permuted, x_low, y_low)], *weights, 1, groups)
-    permuted = after(permuted, xy_top, xy_low)
+    first = token_exchange(shards)
+    bufs = with_cores(near1, far1, corner1)
+    bufs[-1] = after(bufs[-1], permuted)
+    permuted, shards = project(place, bufs, *weights, 1, groups)
+    second = token_exchange(after(shard, *first) for shard in shards)
     placed = reorder(block_order, after(sent, permuted, *first), block)
     sent = exchange(permuted.reshape(devices, rows // devices, units), "tensor")
-    second = [shard if m == 0 else swap(after(shard, permuted, *first), "dp", m) for m, shard in enumerate(shards)]
-    mine = [piece for pair in zip(first, second) for piece in pair]
     returned = exchange(after(placed, sent), "tensor").reshape(rows, units)
-    placed = reorder(block_order, after(sent, placed, *mine), block)
-    theirs = [swap(value, "tensor", 1) for value in mine]
-    values = [quantized, x_top, x_low, y_top, y_low, xy_top, xy_low]
-    grad_weight = weight_rows(core, mine, [quantized, *values[1:-1], after(xy_low, placed)], None)
-    last = exchange(after(placed, returned, grad_weight), "tensor").reshape(rows, units)
-    grad_weight = weight_rows(1 - core, theirs, values, grad_weight)
+    placed = reorder(block_order, after(sent, placed), block)
+    other = [swap(value, "tensor", 1) for value in first]
+    grad_weight = weight_rows(core, group, [after(first[0], placed), *first[1:]], gathered, 0, None)
+    grad_weight = weight_rows(1 - core, group, other, gathered, 0, grad_weight)
+    last = exchange(after(placed, returned, grad_weight, *second), "tensor").reshape(rows, units)
+    other = [swap(value, "tensor", 1) for value in second]
+    grad_weight = weight_rows(core, group, [after(second[0], returned), *second[1:]], gathered, 1, grad_weight)
+    grad_weight = weight_rows(1 - core, group, other, gathered, 1, grad_weight)
     grad_hidden = rotate(returned, first_rot, 0, CHUNKS, None)
     grad_hidden = rotate(last, first_rot, 1, CHUNKS, grad_hidden)
     return (grad_hidden, grad_weight)

time: 305 us -> 279 us (0.915)
  waiting for transfers between devices: 127 us -> 86.8 us
  Pallas kernels: 115 us -> 128 us
    all_gather x2 -> x1, waiting for transfers between devices: 30.1 us -> 0.01 us  [per_device(): lax.all_gather(quantized.reshape(CHUNKS, rows, units), 'dp', axis=0)]
    pallas_call x2 -> x4, Pallas kernels: 39.1 us -> 52.7 us  [weight_rows(): pl.pallas_call(kernel, grid_spec=pltpu.PrefetchScalarGridSpec(num_scalar_...]
    ppermute x20 -> x27, waiting for transfers between devices: 83.7 us -> 72.1 us  [swap(): return lax.ppermute(values, axis, [(t, t ^ bits) for t in range(size)])]
    slice x2 -> x1, local copies, waits for them, and re-layouts: 4.28 us -> 0.86 us  [per_device(): own = (grad_out[:rows], grad_out[rows:])]
    ppermute x20 -> x27, starting transfers between devices: 18.8 us -> 21.7 us  [swap(): return lax.ppermute(values, axis, [(t, t ^ bits) for t in range(size)])]
    unnamed x36 -> x44, local copies, waits for them, and re-layouts: 6.64 us -> 7.9 us
  transfers between devices with their start and end apart: 26 -> 32, of which waited for: 13 -> 13; matrix products, arithmetic and copies ran while one was open for 1% -> 1% of each run, Pallas kernels for 36% -> 45%
where the time goes in v1:
time: 279 us; the launch traced here: 277 us
  Pallas kernels  128 us (46%)
  waiting for transfers between devices  86.8 us (31%)
  starting transfers between devices  38 us (14%)
  between operations  14.2 us (5%)
  local copies, waits for them, and re-layouts  8.76 us (3%)
    ppermute x27, waiting for transfers between devices, swap(): return lax.ppermute(values, axis, [(t, t ^ bits) for t in range(size)])  72.1 us
    pallas_call x2, Pallas kernels, project(): pl.pallas_call(functools.partial(project_kernel, devices, groups, tile, c...  55 us
    pallas_call x4, Pallas kernels, weight_rows(): pl.pallas_call(kernel, grid_spec=pltpu.PrefetchScalarGridSpec(num_scalar_...  52.7 us
    ppermute x27, starting transfers between devices, swap(): return lax.ppermute(values, axis, [(t, t ^ bits) for t in range(size)])  21.7 us
    all_to_all x4, starting transfers between devices, exchange(): return lax.all_to_all(values, axis, split_axis=0, concat_axis=0, tiled=True)  16.3 us
    all_to_all x4, waiting for transfers between devices, exchange(): return lax.all_to_all(values, axis, split_axis=0, concat_axis=0, tiled=True)  14 us
    pallas_call x2, Pallas kernels, reorder(): pl.pallas_call(functools.partial(reorder_kernel, block), grid_spec=pltpu....  12 us
    pallas_call x2, Pallas kernels, rotate(): pl.pallas_call(rotate_kernel, grid=(units // tile,), in_specs=[pl.BlockSp...  8.01 us
  transfers between devices with their start and end apart: 32, of which 13 were waited for; matrix products, arithmetic and copies ran while one was open for 1% of the time, Pallas kernels for 45%

profile of v1, /device:TPU:0, one launch (start us, length us, event | category | flops | bytes accessed | tf_op | source)
XLA Modules:
  0.0 277.3 jit_solution(12242323944059576988)
XLA Ops:
  9.3 4.0 %collective-permute-start.1 = (bf16[256,1024]{1,0:T(8,128)(2,1)S(1)}, bf16[256,1024]{1,0:T(8,128)(2,1)S(1)}, u32[]{:S(2)}, u32[]{:S(2)}) collective-permute-start(bf16[256,1024]{1,0:T(8,128)(2,1)S(1)} %get-tuple-element.54), channel_id=1, source_target_pairs={{0,4},{1,5},{2,6},{3,7},{4,0},{5,1},{6,2},{7,3},{8,12},{9,13},{10,... | collective-permute-start | bytes 1572872 | tf_op jit(solution)/shard_map/ppermute | solution.py:212
  13.3 1.6 collective-permute-start.2
  14.9 21.7 %collective-permute-done.1.refs_4_ = bf16[256,1024]{1,0:T(8,128)(2,1)S(1)} collective-permute-done((bf16[256,1024]{1,0:T(8,128)(2,1)S(1)}, bf16[256,1024]{1,0:T(8,128)(2,1)S(1)}, u32[]{:S(2)}, u32[]{:S(2)}) %collective-permute-start.1) | collective-permute-done | bytes 524320 | tf_op jit(solution)/shard_map/ppermute | solution.py:212
  36.8 1.5 collective-permute-start.4
  38.3 2.2 collective-permute-start.3
  40.6 18.8 %collective-permute-done.4.refs_6_ = bf16[256,1024]{1,0:T(8,128)(2,1)} collective-permute-done((bf16[256,1024]{1,0:T(8,128)(2,1)S(1)}, bf16[256,1024]{1,0:T(8,128)(2,1)}, u32[]{:S(2)}, u32[]{:S(2)}) %collective-permute-start.4) | collective-permute-done | bytes 524320 | tf_op jit(solution)/shard_map/ppermute | solution.py:212
  60.4 4.6 %collective-permute-done.3.refs_4_ = bf16[256,1024]{1,0:T(8,128)(2,1)S(1)} collective-permute-done((bf16[256,1024]{1,0:T(8,128)(2,1)}, bf16[256,1024]{1,0:T(8,128)(2,1)S(1)}, u32[]{:S(2)}, u32[]{:S(2)}) %collective-permute-start.3) | collective-permute-done | bytes 524320 | tf_op jit(solution)/shard_map/ppermute | solution.py:212
  65.1 2.0 collective-permute-start.8
  68.1 27.5 %shard_map.86 = (bf16[256,3072]{1,0:T(8,128)(2,1)}, bf16[256,1024]{1,0:T(8,128)(2,1)}, bf16[256,1024]{1,0:T(8,128)(2,1)}, bf16[256,1024]{1,0:T(8,128)(2,1)}, bf16[256,1024]{1,0:T(8,128)(2,1)}) custom-call(s32[2]{0:T(128)} %pad_add_fusion.place_ref, bf16[512,1024]{1,0:T(8,128)(2,1)} %refs_0_.3, bf16[512,1024]{1,0:T(8,128)(2,1)} %copy-done.5, ...), custom_call_target="tpu_custom_call" | custom-call | flops 12884901888 | bytes 60817408 | tf_op jit(solution)/shard_map/pallas_call | solution.py:74
  97.3 4.1 %all-to-all-start.1 = ((bf16[8,32,3072]{2,1,0:T(8,128)(2,1)}), bf16[8,32,3072]{2,1,0:T(8,128)(2,1)S(1)}, u32[]{:S(2)}, u32[]{:S(2)}) async-start(bf16[8,32,3072]{2,1,0:T(8,128)(2,1)} %bitcast.12), calls=%async_computation.1 | async-start | bytes 3145728 | tf_op jit(solution)/shard_map/all_to_all | solution.py:216
  102.4 1.2 collective-permute-done.9.refs_7_
  105.9 27.5 %shard_map.87 = (bf16[256,3072]{1,0:T(8,128)(2,1)}, bf16[256,1024]{1,0:T(8,128)(2,1)}, bf16[256,1024]{1,0:T(8,128)(2,1)}, bf16[256,1024]{1,0:T(8,128)(2,1)}, bf16[256,1024]{1,0:T(8,128)(2,1)}) custom-call(s32[2]{0:T(128)} %pad_add_fusion.place_ref, bf16[512,1024]{1,0:T(8,128)(2,1)} %refs_0_.3, bf16[512,1024]{1,0:T(8,128)(2,1)} %copy-done.5, ...), custom_call_target="tpu_custom_call" | custom-call | flops 12884901888 | bytes 60817408 | tf_op jit(solution)/shard_map/pallas_call | solution.py:74
  133.4 5.8 %all-to-all-done.1.in_ref = bf16[8,32,3072]{2,1,0:T(8,128)(2,1)S(1)} async-done(((bf16[8,32,3072]{2,1,0:T(8,128)(2,1)}), bf16[8,32,3072]{2,1,0:T(8,128)(2,1)S(1)}, u32[]{:S(2)}, u32[]{:S(2)}) %all-to-all-start.1) | async-done | bytes 1572896 | tf_op jit(solution)/shard_map/all_to_all | solution.py:216
  139.2 3.6 %all-to-all-start = ((bf16[8,32,3072]{2,1,0:T(8,128)(2,1)}), bf16[8,32,3072]{2,1,0:T(8,128)(2,1)S(1)}, u32[]{:S(2)}, u32[]{:S(2)}) async-start(bf16[8,32,3072]{2,1,0:T(8,128)(2,1)} %bitcast.13), calls=%async_computation | async-start | bytes 3145728 | tf_op jit(solution)/shard_map/all_to_all | solution.py:216
  142.8 1.5 collective-permute-start.13
  144.3 1.5 collective-permute-start.14
  146.3 11.6 %collective-permute-done.13.refs_1_ = bf16[256,1024]{1,0:T(8,128)(2,1)} collective-permute-done((bf16[256,1024]{1,0:T(8,128)(2,1)}, bf16[256,1024]{1,0:T(8,128)(2,1)}, u32[]{:S(2)}, u32[]{:S(2)}) %collective-permute-start.13) | collective-permute-done | bytes 524320 | tf_op jit(solution)/shard_map/ppermute | solution.py:212
  157.9 11.9 %collective-permute-done.14.refs_2_ = bf16[256,1024]{1,0:T(8,128)(2,1)} collective-permute-done((bf16[256,1024]{1,0:T(8,128)(2,1)}, bf16[256,1024]{1,0:T(8,128)(2,1)}, u32[]{:S(2)}, u32[]{:S(2)}) %collective-permute-start.14) | collective-permute-done | bytes 524320 | tf_op jit(solution)/shard_map/ppermute | solution.py:212
  169.8 6.0 %shard_map.88 = bf16[8,32,3072]{2,1,0:T(8,128)(2,1)} custom-call(s32[192]{0:T(256)} %order_ref.3, bf16[8,32,3072]{2,1,0:T(8,128)(2,1)} %copy-done.2), custom_call_target="tpu_custom_call" | custom-call | bytes 3145728 | tf_op jit(solution)/shard_map/pallas_call | solution.py:112
  175.8 4.8 %all-to-all-done.in_ref = bf16[8,32,3072]{2,1,0:T(8,128)(2,1)S(1)} async-done(((bf16[8,32,3072]{2,1,0:T(8,128)(2,1)}), bf16[8,32,3072]{2,1,0:T(8,128)(2,1)S(1)}, u32[]{:S(2)}, u32[]{:S(2)}) %all-to-all-start) | async-done | bytes 1572896 | tf_op jit(solution)/shard_map/all_to_all | solution.py:216
  180.5 3.8 %all-to-all-start.2 = ((bf16[8,32,3072]{2,1,0:T(8,128)(2,1)}), bf16[8,32,3072]{2,1,0:T(8,128)(2,1)S(1)}, u32[]{:S(2)}, u32[]{:S(2)}) async-start(bf16[8,32,3072]{2,1,0:T(8,128)(2,1)} %shard_map.88), calls=%async_computation.2 | async-start | bytes 3145728 | tf_op jit(solution)/shard_map/all_to_all | solution.py:216
  185.8 2.4 collective-permute-start.22
  188.7 6.0 %shard_map.89 = bf16[8,32,3072]{2,1,0:T(8,128)(2,1)} custom-call(s32[192]{0:T(256)} %order_ref.3, bf16[8,32,3072]{2,1,0:T(8,128)(2,1)} %copy-done.1), custom_call_target="tpu_custom_call" | custom-call | bytes 3145728 | tf_op jit(solution)/shard_map/pallas_call | solution.py:112
  194.7 12.7 %shard_map.90.refs_5_ = bf16[2048,3072]{1,0:T(8,128)(2,1)} custom-call(s32[2]{0:T(128)} %pad_add_fusion.2.place_ref, bf16[256,1024]{1,0:T(8,128)(2,1)} %get-tuple-element.43.refs_0_, bf16[256,1024]{1,0:T(8,128)(2,1)} %collective-permute-done.13.refs_1_, bf16[256,1024]{1,0:T(8,128)(2,1)} %collective-permute-done.14.refs_2_, ...), custom_call_target="tpu_custom_call" | custom-call | flops 6442450944 | bytes 20971520 | tf_op jit(solution)/shard_map/pallas_call | solution.py:188
  208.6 12.6 %shard_map.91.refs_5_ = bf16[2048,3072]{1,0:T(8,128)(2,1)} custom-call(s32[2]{0:T(128)} %pad_add_fusion.1.place_ref, bf16[256,1024]{1,0:T(8,128)(2,1)} %collective-permute-done.16.refs_0_, bf16[256,1024]{1,0:T(8,128)(2,1)} %collective-permute-done.17.refs_1_, bf16[256,1024]{1,0:T(8,128)(2,1)} %collective-permute-done.18.refs_2_, ...), custom_call_target="tpu_custom_call", output_to_operand_aliasing={{}: (6, {})} | custom-call | flops 6442450944 | bytes 20971520 | tf_op jit(solution)/shard_map/pallas_call | solution.py:188
  222.7 4.8 %all-to-all-start.3 = ((bf16[8,32,3072]{2,1,0:T(8,128)(2,1)}), bf16[8,32,3072]{2,1,0:T(8,128)(2,1)S(1)}, u32[]{:S(2)}, u32[]{:S(2)}) async-start(bf16[8,32,3072]{2,1,0:T(8,128)(2,1)} %shard_map.89), calls=%async_computation.3 | async-start | bytes 3145728 | tf_op jit(solution)/shard_map/all_to_all | solution.py:216
  228.5 4.0 %shard_map.92.refs_0_ = bf16[512,3072]{1,0:T(8,128)(2,1)} custom-call(bf16[256,3072]{1,0:T(8,128)(2,1)} %bitcast.9, bf16[24,128,128]{2,1,0:T(8,128)(2,1)} %rot_ref.3), custom_call_target="tpu_custom_call" | custom-call | flops 201326592 | bytes 3145728 | tf_op jit(solution)/shard_map/pallas_call | solution.py:141
  232.5 13.7 %shard_map.94.refs_5_ = bf16[2048,3072]{1,0:T(8,128)(2,1)} custom-call(s32[2]{0:T(128)} %pad_add_fusion.2.place_ref, bf16[256,1024]{1,0:T(8,128)(2,1)} %get-tuple-element.53.refs_0_, bf16[256,1024]{1,0:T(8,128)(2,1)} %collective-permute-done.20.refs_1_, bf16[256,1024]{1,0:T(8,128)(2,1)} %copy-done.8, ...), custom_call_target="tpu_custom_call", output_to_operand_aliasing={{}: (6, {})} | custom-call | flops 6442450944 | bytes 20971520 | tf_op jit(solution)/shard_map/pallas_call | solution.py:188
  248.2 13.7 %shard_map.95 = bf16[2048,3072]{1,0:T(8,128)(2,1)} custom-call(s32[2]{0:T(128)} %pad_add_fusion.1.place_ref, bf16[256,1024]{1,0:T(8,128)(2,1)} %copy-done.13, bf16[256,1024]{1,0:T(8,128)(2,1)} %copy-done.17, bf16[256,1024]{1,0:T(8,128)(2,1)} %copy-done.15, bf16[256,1024]{1,0:T(8,128)(2,1)} %copy-done.14, ...), custom_call_target="tpu_custom_call", output_to_operand_aliasing={{}: (6, {})} | custom-call | flops 6442450944 | bytes 20971520 | tf_op jit(solution)/shard_map/pallas_call | solution.py:188
  261.9 3.4 %all-to-all-done.3 = bf16[8,32,3072]{2,1,0:T(8,128)(2,1)S(1)} async-done(((bf16[8,32,3072]{2,1,0:T(8,128)(2,1)}), bf16[8,32,3072]{2,1,0:T(8,128)(2,1)S(1)}, u32[]{:S(2)}, u32[]{:S(2)}) %all-to-all-start.3) | async-done | bytes 1572896 | tf_op jit(solution)/shard_map/all_to_all | solution.py:216
  265.3 1.2 copy-done.4
  266.5 4.0 %shard_map.93 = bf16[512,3072]{1,0:T(8,128)(2,1)} custom-call(bf16[256,3072]{1,0:T(8,128)(2,1)} %bitcast.10, bf16[24,128,128]{2,1,0:T(8,128)(2,1)} %rot_ref.3, bf16[512,3072]{1,0:T(8,128)(2,1)} %shard_map.92.refs_0_), custom_call_target="tpu_custom_call", output_to_operand_aliasing={{}: (2, {})} | custom-call | flops 201326592 | bytes 3145728 | tf_op jit(solution)/shard_map/pallas_call | solution.py:141
  (91 shorter events, 17.5 us)
Async XLA Ops:
  7.2 187.5 %all-gather.2.cloned.1.call-start = ((), (), s32[]{:S(2)}) async-start(), calls=%async_computation.4 | async-start | bytes 15728640 | tf_op jit(solution)/shard_map/all_gather | solution.py:232
  9.3 27.3 %collective-permute-start.1 = (bf16[256,1024]{1,0:T(8,128)(2,1)S(1)}, bf16[256,1024]{1,0:T(8,128)(2,1)S(1)}, u32[]{:S(2)}, u32[]{:S(2)}) collective-permute-start(bf16[256,1024]{1,0:T(8,128)(2,1)S(1)} %get-tuple-element.54), channel_id=1, source_target_pairs={{0,4},{1,5},{2,6},{3,7},{4,0},{5,1},{6,2},{7,3},{8,12},{9,13},{10,... | collective-permute-start | bytes 1572872 | tf_op jit(solution)/shard_map/ppermute | solution.py:212
  13.3 23.6 %collective-permute-start.2 = (bf16[256,1024]{1,0:T(8,128)(2,1)S(1)}, bf16[256,1024]{1,0:T(8,128)(2,1)}, u32[]{:S(2)}, u32[]{:S(2)}) collective-permute-start(bf16[256,1024]{1,0:T(8,128)(2,1)S(1)} %get-tuple-element.54), channel_id=1, source_target_pairs={{0,2},{1,3},{2,0},{3,1},{4,6},{5,7},{6,4},{7,5},{8,10},{9,11},{10,... | collective-permute-start | bytes 1572872 | tf_op jit(solution)/shard_map/ppermute | solution.py:212
  36.8 22.5 %collective-permute-start.4 = (bf16[256,1024]{1,0:T(8,128)(2,1)S(1)}, bf16[256,1024]{1,0:T(8,128)(2,1)}, u32[]{:S(2)}, u32[]{:S(2)}) collective-permute-start(bf16[256,1024]{1,0:T(8,128)(2,1)S(1)} %collective-permute-done.1.refs_4_), channel_id=1, source_target_pairs={{0,2},{1,3},{2,0},{3,1},{4,6},{5,7},{6,4},{7,5},{8,10},{9,11},{10,... | collective-permute-start | bytes 1572872 | tf_op jit(solution)/shard_map/ppermute | solution.py:212
  38.3 28.8 %collective-permute-start = (bf16[512,1024]{1,0:T(8,128)(2,1)S(1)}, bf16[512,1024]{1,0:T(8,128)(2,1)S(1)}, u32[]{:S(2)}, u32[]{:S(2)}) collective-permute-start(bf16[512,1024]{1,0:T(8,128)(2,1)S(1)} %copy-done), channel_id=1, source_target_pairs={{0,1},{1,0},{2,3},{3,2},{4,5},{5,4},{6,7},{7,6},{8,9},{9,8},{10,11... | collective-permute-start | bytes 3145736 | tf_op jit(solution)/shard_map/ppermute | solution.py:212
  38.3 26.7 %collective-permute-start.3 = (bf16[256,1024]{1,0:T(8,128)(2,1)}, bf16[256,1024]{1,0:T(8,128)(2,1)S(1)}, u32[]{:S(2)}, u32[]{:S(2)}) collective-permute-start(bf16[256,1024]{1,0:T(8,128)(2,1)} %get-tuple-element.30), channel_id=1, source_target_pairs={{0,4},{1,5},{2,6},{3,7},{4,0},{5,1},{6,2},{7,3},{8,12},{9,13},{10,... | collective-permute-start | bytes 1572872 | tf_op jit(solution)/shard_map/ppermute | solution.py:212
  59.3 5.8 %collective-permute-start.12 = (bf16[256,1024]{1,0:T(8,128)(2,1)}, bf16[256,1024]{1,0:T(8,128)(2,1)}, u32[]{:S(2)}, u32[]{:S(2)}) collective-permute-start(bf16[256,1024]{1,0:T(8,128)(2,1)} %collective-permute-done.4.refs_6_), channel_id=1, source_target_pairs={{0,1},{1,0},{2,3},{3,2},{4,5},{5,4},{6,7},{7,6},{8,9},{9,8},{10,11... | collective-permute-start | bytes 1572872 | tf_op jit(solution)/shard_map/ppermute | solution.py:212
  59.3 7.8 %collective-permute-start.10 = (bf16[256,1024]{1,0:T(8,128)(2,1)}, bf16[256,1024]{1,0:T(8,128)(2,1)}, u32[]{:S(2)}, u32[]{:S(2)}) collective-permute-start(bf16[256,1024]{1,0:T(8,128)(2,1)} %collective-permute-done.2.refs_2_), channel_id=1, source_target_pairs={{0,1},{1,0},{2,3},{3,2},{4,5},{5,4},{6,7},{7,6},{8,9},{9,8},{10,11... | collective-permute-start | bytes 1572872 | tf_op jit(solution)/shard_map/ppermute | solution.py:212
  59.8 7.3 %collective-permute-start.11 = (bf16[256,1024]{1,0:T(8,128)(2,1)S(1)}, bf16[256,1024]{1,0:T(8,128)(2,1)}, u32[]{:S(2)}, u32[]{:S(2)}) collective-permute-start(bf16[256,1024]{1,0:T(8,128)(2,1)S(1)} %collective-permute-done.1.refs_4_), channel_id=1, source_target_pairs={{0,1},{1,0},{2,3},{3,2},{4,5},{5,4},{6,7},{7,6},{8,9},{9,8},{10,11... | collective-permute-start | bytes 1572872 | tf_op jit(solution)/shard_map/ppermute | solution.py:212
  65.1 30.6 %collective-permute-start.5 = (bf16[256,1024]{1,0:T(8,128)(2,1)}, bf16[256,1024]{1,0:T(8,128)(2,1)S(1)}, u32[]{:S(2)}, u32[]{:S(2)}) collective-permute-start(bf16[256,1024]{1,0:T(8,128)(2,1)} %get-tuple-element.30), channel_id=1, source_target_pairs={{0,2},{1,3},{2,0},{3,1},{4,6},{5,7},{6,4},{7,5},{8,10},{9,11},{10,... | collective-permute-start | bytes 1572872 | tf_op jit(solution)/shard_map/ppermute | solution.py:212
  65.1 30.6 %collective-permute-start.8 = (bf16[256,1024]{1,0:T(8,128)(2,1)S(1)}, bf16[256,1024]{1,0:T(8,128)(2,1)S(1)}, u32[]{:S(2)}, u32[]{:S(2)}) collective-permute-start(bf16[256,1024]{1,0:T(8,128)(2,1)S(1)} %collective-permute-done.3.refs_4_), channel_id=1, source_target_pairs={{0,2},{1,3},{2,0},{3,1},{4,6},{5,7},{6,4},{7,5},{8,10},{9,11},{10,... | collective-permute-start | bytes 1572872 | tf_op jit(solution)/shard_map/ppermute | solution.py:212
  97.3 41.9 %all-to-all-start.1 = ((bf16[8,32,3072]{2,1,0:T(8,128)(2,1)}), bf16[8,32,3072]{2,1,0:T(8,128)(2,1)S(1)}, u32[]{:S(2)}, u32[]{:S(2)}) async-start(bf16[8,32,3072]{2,1,0:T(8,128)(2,1)} %bitcast.12), calls=%async_computation.1 | async-start | bytes 3145728 | tf_op jit(solution)/shard_map/all_to_all | solution.py:216
  101.4 2.2 collective-permute-start.9
  101.9 2.4 collective-permute-start.7
  102.0 3.1 %collective-permute-start.6 = (bf16[256,1024]{1,0:T(8,128)(2,1)S(1)}, bf16[256,1024]{1,0:T(8,128)(2,1)S(1)}, u32[]{:S(2)}, u32[]{:S(2)}) collective-permute-start(bf16[256,1024]{1,0:T(8,128)(2,1)S(1)} %copy-done.10), channel_id=1, source_target_pairs={{0,1},{1,0},{2,3},{3,2},{4,5},{5,4},{6,7},{7,6},{8,9},{9,8},{10,11... | collective-permute-start | bytes 1572872 | tf_op jit(solution)/shard_map/ppermute | solution.py:212
  139.2 41.3 %all-to-all-start = ((bf16[8,32,3072]{2,1,0:T(8,128)(2,1)}), bf16[8,32,3072]{2,1,0:T(8,128)(2,1)S(1)}, u32[]{:S(2)}, u32[]{:S(2)}) async-start(bf16[8,32,3072]{2,1,0:T(8,128)(2,1)} %bitcast.13), calls=%async_computation | async-start | bytes 3145728 | tf_op jit(solution)/shard_map/all_to_all | solution.py:216
  142.8 15.1 %collective-permute-start.13 = (bf16[256,1024]{1,0:T(8,128)(2,1)}, bf16[256,1024]{1,0:T(8,128)(2,1)}, u32[]{:S(2)}, u32[]{:S(2)}) collective-permute-start(bf16[256,1024]{1,0:T(8,128)(2,1)} %get-tuple-element.37), channel_id=1, source_target_pairs={{0,8},{8,0},{16,24},{24,16},{1,9},{9,1},{17,25},{25,17},{2,10},{10... | collective-permute-start | bytes 1572872 | tf_op jit(solution)/shard_map/ppermute | solution.py:212
  144.3 25.4 %collective-permute-start.14 = (bf16[256,1024]{1,0:T(8,128)(2,1)}, bf16[256,1024]{1,0:T(8,128)(2,1)}, u32[]{:S(2)}, u32[]{:S(2)}) collective-permute-start(bf16[256,1024]{1,0:T(8,128)(2,1)} %get-tuple-element.38), channel_id=1, source_target_pairs={{0,16},{8,24},{16,0},{24,8},{1,17},{9,25},{17,1},{25,9},{2,18},{10... | collective-permute-start | bytes 1572872 | tf_op jit(solution)/shard_map/ppermute | solution.py:212
  145.8 23.9 %collective-permute-start.15 = (bf16[256,1024]{1,0:T(8,128)(2,1)}, bf16[256,1024]{1,0:T(8,128)(2,1)}, u32[]{:S(2)}, u32[]{:S(2)}) collective-permute-start(bf16[256,1024]{1,0:T(8,128)(2,1)} %get-tuple-element.39), channel_id=1, source_target_pairs={{0,24},{8,16},{16,8},{24,0},{1,25},{9,17},{17,9},{25,1},{2,26},{10... | collective-permute-start | bytes 1572872 | tf_op jit(solution)/shard_map/ppermute | solution.py:212
  180.5 42.1 %all-to-all-start.2 = ((bf16[8,32,3072]{2,1,0:T(8,128)(2,1)}), bf16[8,32,3072]{2,1,0:T(8,128)(2,1)S(1)}, u32[]{:S(2)}, u32[]{:S(2)}) async-start(bf16[8,32,3072]{2,1,0:T(8,128)(2,1)} %shard_map.88), calls=%async_computation.2 | async-start | bytes 3145728 | tf_op jit(solution)/shard_map/all_to_all | solution.py:216
  185.6 21.9 %collective-permute-start.16 = (bf16[256,1024]{1,0:T(8,128)(2,1)}, bf16[256,1024]{1,0:T(8,128)(2,1)}, u32[]{:S(2)}, u32[]{:S(2)}) collective-permute-start(bf16[256,1024]{1,0:T(8,128)(2,1)} %get-tuple-element.43.refs_0_), channel_id=1, source_target_pairs={{0,1},{1,0},{2,3},{3,2},{4,5},{5,4},{6,7},{7,6},{8,9},{9,8},{10,11... | collective-permute-start | bytes 1572872 | tf_op jit(solution)/shard_map/ppermute | solution.py:212
  185.8 35.4 %collective-permute-start.22 = (bf16[256,1024]{1,0:T(8,128)(2,1)}, bf16[256,1024]{1,0:T(8,128)(2,1)}, u32[]{:S(2)}, u32[]{:S(2)}) collective-permute-start(bf16[256,1024]{1,0:T(8,128)(2,1)} %get-tuple-element.51), channel_id=1, source_target_pairs={{0,24},{8,16},{16,8},{24,0},{1,25},{9,17},{17,9},{25,1},{2,26},{10... | collective-permute-start | bytes 1572872 | tf_op jit(solution)/shard_map/ppermute | solution.py:212
  188.2 19.9 %collective-permute-start.17 = (bf16[256,1024]{1,0:T(8,128)(2,1)}, bf16[256,1024]{1,0:T(8,128)(2,1)}, u32[]{:S(2)}, u32[]{:S(2)}) collective-permute-start(bf16[256,1024]{1,0:T(8,128)(2,1)} %collective-permute-done.13.refs_1_), channel_id=1, source_target_pairs={{0,1},{1,0},{2,3},{3,2},{4,5},{5,4},{6,7},{7,6},{8,9},{9,8},{10,11... | collective-permute-start | bytes 1572872 | tf_op jit(solution)/shard_map/ppermute | solution.py:212
  188.2 20.4 %collective-permute-start.18 = (bf16[256,1024]{1,0:T(8,128)(2,1)}, bf16[256,1024]{1,0:T(8,128)(2,1)}, u32[]{:S(2)}, u32[]{:S(2)}) collective-permute-start(bf16[256,1024]{1,0:T(8,128)(2,1)} %collective-permute-done.14.refs_2_), channel_id=1, source_target_pairs={{0,1},{1,0},{2,3},{3,2},{4,5},{5,4},{6,7},{7,6},{8,9},{9,8},{10,11... | collective-permute-start | bytes 1572872 | tf_op jit(solution)/shard_map/ppermute | solution.py:212
  188.7 19.9 %collective-permute-start.19 = (bf16[256,1024]{1,0:T(8,128)(2,1)}, bf16[256,1024]{1,0:T(8,128)(2,1)}, u32[]{:S(2)}, u32[]{:S(2)}) collective-permute-start(bf16[256,1024]{1,0:T(8,128)(2,1)} %collective-permute-done.15.refs_3_), channel_id=1, source_target_pairs={{0,1},{1,0},{2,3},{3,2},{4,5},{5,4},{6,7},{7,6},{8,9},{9,8},{10,11... | collective-permute-start | bytes 1572872 | tf_op jit(solution)/shard_map/ppermute | solution.py:212
  207.5 14.4 %collective-permute-start.21 = (bf16[256,1024]{1,0:T(8,128)(2,1)S(1)}, bf16[256,1024]{1,0:T(8,128)(2,1)S(1)}, u32[]{:S(2)}, u32[]{:S(2)}) collective-permute-start(bf16[256,1024]{1,0:T(8,128)(2,1)S(1)} %copy-done.21), channel_id=1, source_target_pairs={{0,16},{8,24},{16,0},{24,8},{1,17},{9,25},{17,1},{25,9},{2,18},{10... | collective-permute-start | bytes 1572872 | tf_op jit(solution)/shard_map/ppermute | solution.py:212
  208.0 14.6 %collective-permute-start.20 = (bf16[256,1024]{1,0:T(8,128)(2,1)S(1)}, bf16[256,1024]{1,0:T(8,128)(2,1)}, u32[]{:S(2)}, u32[]{:S(2)}) collective-permute-start(bf16[256,1024]{1,0:T(8,128)(2,1)S(1)} %copy-done.20), channel_id=1, source_target_pairs={{0,8},{8,0},{16,24},{24,16},{1,9},{9,1},{17,25},{25,17},{2,10},{10... | collective-permute-start | bytes 1572872 | tf_op jit(solution)/shard_map/ppermute | solution.py:212
  222.7 42.6 %all-to-all-start.3 = ((bf16[8,32,3072]{2,1,0:T(8,128)(2,1)}), bf16[8,32,3072]{2,1,0:T(8,128)(2,1)S(1)}, u32[]{:S(2)}, u32[]{:S(2)}) async-start(bf16[8,32,3072]{2,1,0:T(8,128)(2,1)} %shard_map.89), calls=%async_computation.3 | async-start | bytes 3145728 | tf_op jit(solution)/shard_map/all_to_all | solution.py:216
  227.5 18.7 %collective-permute-start.23 = (bf16[256,1024]{1,0:T(8,128)(2,1)}, bf16[256,1024]{1,0:T(8,128)(2,1)S(1)}, u32[]{:S(2)}, u32[]{:S(2)}) collective-permute-start(bf16[256,1024]{1,0:T(8,128)(2,1)} %get-tuple-element.53.refs_0_), channel_id=1, source_target_pairs={{0,1},{1,0},{2,3},{3,2},{4,5},{5,4},{6,7},{7,6},{8,9},{9,8},{10,11... | collective-permute-start | bytes 1572872 | tf_op jit(solution)/shard_map/ppermute | solution.py:212
  228.0 18.2 %collective-permute-start.26 = (bf16[256,1024]{1,0:T(8,128)(2,1)}, bf16[256,1024]{1,0:T(8,128)(2,1)S(1)}, u32[]{:S(2)}, u32[]{:S(2)}) collective-permute-start(bf16[256,1024]{1,0:T(8,128)(2,1)} %collective-permute-done.22.refs_3_), channel_id=1, source_target_pairs={{0,1},{1,0},{2,3},{3,2},{4,5},{5,4},{6,7},{7,6},{8,9},{9,8},{10,11... | collective-permute-start | bytes 1572872 | tf_op jit(solution)/shard_map/ppermute | solution.py:212
  228.0 18.2 %collective-permute-start.25 = (bf16[256,1024]{1,0:T(8,128)(2,1)}, bf16[256,1024]{1,0:T(8,128)(2,1)S(1)}, u32[]{:S(2)}, u32[]{:S(2)}) collective-permute-start(bf16[256,1024]{1,0:T(8,128)(2,1)} %copy-done.8), channel_id=1, source_target_pairs={{0,1},{1,0},{2,3},{3,2},{4,5},{5,4},{6,7},{7,6},{8,9},{9,8},{10,11... | collective-permute-start | bytes 1572872 | tf_op jit(solution)/shard_map/ppermute | solution.py:212
  228.5 17.8 %collective-permute-start.24 = (bf16[256,1024]{1,0:T(8,128)(2,1)}, bf16[256,1024]{1,0:T(8,128)(2,1)S(1)}, u32[]{:S(2)}, u32[]{:S(2)}) collective-permute-start(bf16[256,1024]{1,0:T(8,128)(2,1)} %collective-permute-done.20.refs_1_), channel_id=1, source_target_pairs={{0,1},{1,0},{2,3},{3,2},{4,5},{5,4},{6,7},{7,6},{8,9},{9,8},{10,11... | collective-permute-start | bytes 1572872 | tf_op jit(solution)/shard_map/ppermute | solution.py:212
  (22 other events, 159.5 us)
Sparse Core Ops, SparseCore 0:
  9.8 125.2 all-gather.1

commit v2 on v1

--- a/solution.py
+++ b/solution.py
@@ -235,16 +235,15 @@
     whole = swap(grad_out, "tensor", 1)
     far0, near0 = swap(own[0], "tensor", 4), swap(own[0], "tensor", 2)
     corner0 = swap(after(far0, near0), "tensor", 2)
-    far1 = swap(after(own[1], far0, near0), "tensor", 4)
-    corner1, near1 = swap(far1, "tensor", 2), swap(after(own[1], far1, corner0), "tensor", 2)
+    far1 = swap(after(own[1], corner0), "tensor", 4)
+    corner1, near1 = swap(far1, "tensor", 2), swap(after(own[1], corner0), "tensor", 2)
 
     def with_cores(near, far, corner):
         return [grad_out, whole] + [buf for values in (near, far, corner) for buf in (values, swap(values, "tensor", 1))]
 
     bufs = with_cores(near0, far0, corner0)
-    bufs[-1] = after(bufs[-1], far1)
     permuted, shards = project(place, bufs, *weights, 0, groups)
-    permuted = after(permuted, near1, corner1)
+    permuted = after(permuted, near1, far1)
     sent = exchange(permuted.reshape(devices, rows // devices, units), "tensor")
     first = token_exchange(shards)
     bufs = with_cores(near1, far1, corner1)

time: 279 us -> 300 us (1.075)
  waiting for transfers between devices: 86.8 us -> 106 us
    ppermute x27, waiting for transfers between devices: 72.1 us -> 97.7 us  [swap(): return lax.ppermute(values, axis, [(t, t ^ bits) for t in range(size)])]
    all_to_all x4, waiting for transfers between devices: 14 us -> 7.97 us  [exchange(): return lax.all_to_all(values, axis, split_axis=0, concat_axis=0, tiled=True)]
    unnamed x44 -> x38, local copies, waits for them, and re-layouts: 7.9 us -> 6.76 us
  transfers between devices with their start and end apart: 32 -> 32, of which waited for: 13 -> 12; matrix products, arithmetic and copies ran while one was open for 1% -> 1% of each run, Pallas kernels for 45% -> 42%
where the time goes in v2:
time: 300 us; the launch traced here: 298 us
  Pallas kernels  128 us (43%)
  waiting for transfers between devices  106 us (35%)
  starting transfers between devices  39.9 us (13%)
  between operations  14.2 us (5%)
  local copies, waits for them, and re-layouts  7.62 us (3%)
    ppermute x27, waiting for transfers between devices, swap(): return lax.ppermute(values, axis, [(t, t ^ bits) for t in range(size)])  97.7 us
    pallas_call x2, Pallas kernels, project(): pl.pallas_call(functools.partial(project_kernel, devices, groups, tile, c...  55.6 us
    pallas_call x4, Pallas kernels, weight_rows(): pl.pallas_call(kernel, grid_spec=pltpu.PrefetchScalarGridSpec(num_scalar_...  52.7 us
    ppermute x27, starting transfers between devices, swap(): return lax.ppermute(values, axis, [(t, t ^ bits) for t in range(size)])  23.9 us
    all_to_all x4, starting transfers between devices, exchange(): return lax.all_to_all(values, axis, split_axis=0, concat_axis=0, tiled=True)  15.9 us
    pallas_call x2, Pallas kernels, reorder(): pl.pallas_call(functools.partial(reorder_kernel, block), grid_spec=pltpu....  12 us
    pallas_call x2, Pallas kernels, rotate(): pl.pallas_call(rotate_kernel, grid=(units // tile,), in_specs=[pl.BlockSp...  8.02 us
    all_to_all x4, waiting for transfers between devices, exchange(): return lax.all_to_all(values, axis, split_axis=0, concat_axis=0, tiled=True)  7.97 us
  transfers between devices with their start and end apart: 32, of which 12 were waited for; matrix products, arithmetic and copies ran while one was open for 1% of the time, Pallas kernels for 42%

profile of v2, /device:TPU:0, one launch (start us, length us, event | category | flops | bytes accessed | tf_op | source)
XLA Modules:
  0.0 298.2 jit_solution(16873854107708579739)
XLA Ops:
  9.3 4.0 %collective-permute-start.1 = (bf16[256,1024]{1,0:T(8,128)(2,1)S(1)}, bf16[256,1024]{1,0:T(8,128)(2,1)S(1)}, u32[]{:S(2)}, u32[]{:S(2)}) collective-permute-start(bf16[256,1024]{1,0:T(8,128)(2,1)S(1)} %get-tuple-element.50), channel_id=1, source_target_pairs={{0,4},{1,5},{2,6},{3,7},{4,0},{5,1},{6,2},{7,3},{8,12},{9,13},{10,... | collective-permute-start | bytes 1572872 | tf_op jit(solution)/shard_map/ppermute | solution.py:212
  13.3 1.6 collective-permute-start.2
  14.9 21.7 %collective-permute-done.1.refs_4_ = bf16[256,1024]{1,0:T(8,128)(2,1)S(1)} collective-permute-done((bf16[256,1024]{1,0:T(8,128)(2,1)S(1)}, bf16[256,1024]{1,0:T(8,128)(2,1)S(1)}, u32[]{:S(2)}, u32[]{:S(2)}) %collective-permute-start.1) | collective-permute-done | bytes 524320 | tf_op jit(solution)/shard_map/ppermute | solution.py:212
  36.8 1.5 collective-permute-start.3
  38.8 10.9 %collective-permute-done.3.refs_6_ = bf16[256,1024]{1,0:T(8,128)(2,1)} collective-permute-done((bf16[256,1024]{1,0:T(8,128)(2,1)S(1)}, bf16[256,1024]{1,0:T(8,128)(2,1)}, u32[]{:S(2)}, u32[]{:S(2)}) %collective-permute-start.3) | collective-permute-done | bytes 524320 | tf_op jit(solution)/shard_map/ppermute | solution.py:212
  50.3 3.0 %collective-permute-start.6 = (bf16[256,1024]{1,0:T(8,128)(2,1)}, bf16[256,1024]{1,0:T(8,128)(2,1)S(1)}, u32[]{:S(2)}, u32[]{:S(2)}) collective-permute-start(bf16[256,1024]{1,0:T(8,128)(2,1)} %get-tuple-element.27), channel_id=1, source_target_pairs={{0,4},{1,5},{2,6},{3,7},{4,0},{5,1},{6,2},{7,3},{8,12},{9,13},{10,... | collective-permute-start | bytes 1572872 | tf_op jit(solution)/shard_map/ppermute | solution.py:212
  53.4 1.7 collective-permute-start.4
  56.1 28.1 %shard_map.86 = (bf16[256,3072]{1,0:T(8,128)(2,1)}, bf16[256,1024]{1,0:T(8,128)(2,1)}, bf16[256,1024]{1,0:T(8,128)(2,1)}, bf16[256,1024]{1,0:T(8,128)(2,1)}, bf16[256,1024]{1,0:T(8,128)(2,1)}) custom-call(s32[2]{0:T(128)} %pad_add_fusion.place_ref, bf16[512,1024]{1,0:T(8,128)(2,1)} %refs_0_.3, bf16[512,1024]{1,0:T(8,128)(2,1)} %copy-done.5, ...), custom_call_target="tpu_custom_call" | custom-call | flops 12884901888 | bytes 60817408 | tf_op jit(solution)/shard_map/pallas_call | solution.py:74
  84.2 3.6 %all-to-all-start.1 = ((bf16[8,32,3072]{2,1,0:T(8,128)(2,1)}), bf16[8,32,3072]{2,1,0:T(8,128)(2,1)S(1)}, u32[]{:S(2)}, u32[]{:S(2)}) async-start(bf16[8,32,3072]{2,1,0:T(8,128)(2,1)} %bitcast.12), calls=%async_computation.1 | async-start | bytes 3145728 | tf_op jit(solution)/shard_map/all_to_all | solution.py:216
  87.8 1.9 collective-permute-start.8
  89.7 37.7 %collective-permute-done.8.refs_6_ = bf16[256,1024]{1,0:T(8,128)(2,1)S(1)} collective-permute-done((bf16[256,1024]{1,0:T(8,128)(2,1)S(1)}, bf16[256,1024]{1,0:T(8,128)(2,1)S(1)}, u32[]{:S(2)}, u32[]{:S(2)}) %collective-permute-start.8) | collective-permute-done | bytes 524320 | tf_op jit(solution)/shard_map/ppermute | solution.py:212
  128.0 1.4 collective-permute-done.9.refs_7_
  129.4 1.5 collective-permute-done.7.refs_5_
  132.5 27.5 %shard_map.87 = (bf16[256,3072]{1,0:T(8,128)(2,1)}, bf16[256,1024]{1,0:T(8,128)(2,1)}, bf16[256,1024]{1,0:T(8,128)(2,1)}, bf16[256,1024]{1,0:T(8,128)(2,1)}, bf16[256,1024]{1,0:T(8,128)(2,1)}) custom-call(s32[2]{0:T(128)} %pad_add_fusion.place_ref, bf16[512,1024]{1,0:T(8,128)(2,1)} %refs_0_.3, bf16[512,1024]{1,0:T(8,128)(2,1)} %copy-done.5, ...), custom_call_target="tpu_custom_call" | custom-call | flops 12884901888 | bytes 60817408 | tf_op jit(solution)/shard_map/pallas_call | solution.py:74
  160.0 3.7 %all-to-all-start = ((bf16[8,32,3072]{2,1,0:T(8,128)(2,1)}), bf16[8,32,3072]{2,1,0:T(8,128)(2,1)S(1)}, u32[]{:S(2)}, u32[]{:S(2)}) async-start(bf16[8,32,3072]{2,1,0:T(8,128)(2,1)} %bitcast.13), calls=%async_computation | async-start | bytes 3145728 | tf_op jit(solution)/shard_map/all_to_all | solution.py:216
  163.8 1.6 collective-permute-start.13
  165.4 1.5 collective-permute-start.14
  167.2 11.5 %collective-permute-done.13.refs_1_ = bf16[256,1024]{1,0:T(8,128)(2,1)} collective-permute-done((bf16[256,1024]{1,0:T(8,128)(2,1)}, bf16[256,1024]{1,0:T(8,128)(2,1)}, u32[]{:S(2)}, u32[]{:S(2)}) %collective-permute-start.13) | collective-permute-done | bytes 524320 | tf_op jit(solution)/shard_map/ppermute | solution.py:212
  178.8 12.2 %collective-permute-done.14.refs_2_ = bf16[256,1024]{1,0:T(8,128)(2,1)} collective-permute-done((bf16[256,1024]{1,0:T(8,128)(2,1)}, bf16[256,1024]{1,0:T(8,128)(2,1)}, u32[]{:S(2)}, u32[]{:S(2)}) %collective-permute-start.14) | collective-permute-done | bytes 524320 | tf_op jit(solution)/shard_map/ppermute | solution.py:212
  191.0 6.1 %shard_map.88 = bf16[8,32,3072]{2,1,0:T(8,128)(2,1)} custom-call(s32[192]{0:T(256)} %order_ref.3, bf16[8,32,3072]{2,1,0:T(8,128)(2,1)} %copy-done.2), custom_call_target="tpu_custom_call" | custom-call | bytes 3145728 | tf_op jit(solution)/shard_map/pallas_call | solution.py:112
  197.1 4.5 %all-to-all-done.in_ref = bf16[8,32,3072]{2,1,0:T(8,128)(2,1)S(1)} async-done(((bf16[8,32,3072]{2,1,0:T(8,128)(2,1)}), bf16[8,32,3072]{2,1,0:T(8,128)(2,1)S(1)}, u32[]{:S(2)}, u32[]{:S(2)}) %all-to-all-start) | async-done | bytes 1572896 | tf_op jit(solution)/shard_map/all_to_all | solution.py:216
  201.6 3.8 %all-to-all-start.2 = ((bf16[8,32,3072]{2,1,0:T(8,128)(2,1)}), bf16[8,32,3072]{2,1,0:T(8,128)(2,1)S(1)}, u32[]{:S(2)}, u32[]{:S(2)}) async-start(bf16[8,32,3072]{2,1,0:T(8,128)(2,1)} %shard_map.88), calls=%async_computation.2 | async-start | bytes 3145728 | tf_op jit(solution)/shard_map/all_to_all | solution.py:216
  207.6 2.6 collective-permute-start.22
  210.2 6.0 %shard_map.89 = bf16[8,32,3072]{2,1,0:T(8,128)(2,1)} custom-call(s32[192]{0:T(256)} %order_ref.3, bf16[8,32,3072]{2,1,0:T(8,128)(2,1)} %copy-done.1), custom_call_target="tpu_custom_call" | custom-call | bytes 3145728 | tf_op jit(solution)/shard_map/pallas_call | solution.py:112
  216.2 12.7 %shard_map.90.refs_5_ = bf16[2048,3072]{1,0:T(8,128)(2,1)} custom-call(s32[2]{0:T(128)} %pad_add_fusion.2.place_ref, bf16[256,1024]{1,0:T(8,128)(2,1)} %get-tuple-element.39.refs_0_, bf16[256,1024]{1,0:T(8,128)(2,1)} %collective-permute-done.13.refs_1_, bf16[256,1024]{1,0:T(8,128)(2,1)} %collective-permute-done.14.refs_2_, ...), custom_call_target="tpu_custom_call" | custom-call | flops 6442450944 | bytes 20971520 | tf_op jit(solution)/shard_map/pallas_call | solution.py:188
  229.9 12.6 %shard_map.91.refs_5_ = bf16[2048,3072]{1,0:T(8,128)(2,1)} custom-call(s32[2]{0:T(128)} %pad_add_fusion.1.place_ref, bf16[256,1024]{1,0:T(8,128)(2,1)} %collective-permute-done.16.refs_0_, bf16[256,1024]{1,0:T(8,128)(2,1)} %collective-permute-done.17.refs_1_, bf16[256,1024]{1,0:T(8,128)(2,1)} %collective-permute-done.18.refs_2_, ...), custom_call_target="tpu_custom_call", output_to_operand_aliasing={{}: (6, {})} | custom-call | flops 6442450944 | bytes 20971520 | tf_op jit(solution)/shard_map/pallas_call | solution.py:188
  243.6 4.8 %all-to-all-start.3 = ((bf16[8,32,3072]{2,1,0:T(8,128)(2,1)}), bf16[8,32,3072]{2,1,0:T(8,128)(2,1)S(1)}, u32[]{:S(2)}, u32[]{:S(2)}) async-start(bf16[8,32,3072]{2,1,0:T(8,128)(2,1)} %shard_map.89), calls=%async_computation.3 | async-start | bytes 3145728 | tf_op jit(solution)/shard_map/all_to_all | solution.py:216
  249.4 4.0 %shard_map.92.refs_0_ = bf16[512,3072]{1,0:T(8,128)(2,1)} custom-call(bf16[256,3072]{1,0:T(8,128)(2,1)} %bitcast.9, bf16[24,128,128]{2,1,0:T(8,128)(2,1)} %rot_ref.3), custom_call_target="tpu_custom_call" | custom-call | flops 201326592 | bytes 3145728 | tf_op jit(solution)/shard_map/pallas_call | solution.py:141
  253.4 13.7 %shard_map.94.refs_5_ = bf16[2048,3072]{1,0:T(8,128)(2,1)} custom-call(s32[2]{0:T(128)} %pad_add_fusion.2.place_ref, bf16[256,1024]{1,0:T(8,128)(2,1)} %get-tuple-element.49.refs_0_, bf16[256,1024]{1,0:T(8,128)(2,1)} %collective-permute-done.20.refs_1_, bf16[256,1024]{1,0:T(8,128)(2,1)} %copy-done.8, ...), custom_call_target="tpu_custom_call", output_to_operand_aliasing={{}: (6, {})} | custom-call | flops 6442450944 | bytes 20971520 | tf_op jit(solution)/shard_map/pallas_call | solution.py:188
  269.1 13.7 %shard_map.95 = bf16[2048,3072]{1,0:T(8,128)(2,1)} custom-call(s32[2]{0:T(128)} %pad_add_fusion.1.place_ref, bf16[256,1024]{1,0:T(8,128)(2,1)} %copy-done.9, bf16[256,1024]{1,0:T(8,128)(2,1)} %copy-done.14, bf16[256,1024]{1,0:T(8,128)(2,1)} %copy-done.12, bf16[256,1024]{1,0:T(8,128)(2,1)} %copy-done.11, ...), custom_call_target="tpu_custom_call", output_to_operand_aliasing={{}: (6, {})} | custom-call | flops 6442450944 | bytes 20971520 | tf_op jit(solution)/shard_map/pallas_call | solution.py:188
  282.8 3.4 %all-to-all-done.3 = bf16[8,32,3072]{2,1,0:T(8,128)(2,1)S(1)} async-done(((bf16[8,32,3072]{2,1,0:T(8,128)(2,1)}), bf16[8,32,3072]{2,1,0:T(8,128)(2,1)S(1)}, u32[]{:S(2)}, u32[]{:S(2)}) %all-to-all-start.3) | async-done | bytes 1572896 | tf_op jit(solution)/shard_map/all_to_all | solution.py:216
  287.4 4.0 %shard_map.93 = bf16[512,3072]{1,0:T(8,128)(2,1)} custom-call(bf16[256,3072]{1,0:T(8,128)(2,1)} %bitcast.10, bf16[24,128,128]{2,1,0:T(8,128)(2,1)} %rot_ref.3, bf16[512,3072]{1,0:T(8,128)(2,1)} %shard_map.92.refs_0_), custom_call_target="tpu_custom_call", output_to_operand_aliasing={{}: (2, {})} | custom-call | flops 201326592 | bytes 3145728 | tf_op jit(solution)/shard_map/pallas_call | solution.py:141
  (85 shorter events, 15.4 us)
Async XLA Ops:
  7.2 209.0 %all-gather.2.cloned.1.call-start = ((), (), s32[]{:S(2)}) async-start(), calls=%async_computation.4 | async-start | bytes 15728640 | tf_op jit(solution)/shard_map/all_gather | solution.py:232
  9.3 27.3 %collective-permute-start.1 = (bf16[256,1024]{1,0:T(8,128)(2,1)S(1)}, bf16[256,1024]{1,0:T(8,128)(2,1)S(1)}, u32[]{:S(2)}, u32[]{:S(2)}) collective-permute-start(bf16[256,1024]{1,0:T(8,128)(2,1)S(1)} %get-tuple-element.50), channel_id=1, source_target_pairs={{0,4},{1,5},{2,6},{3,7},{4,0},{5,1},{6,2},{7,3},{8,12},{9,13},{10,... | collective-permute-start | bytes 1572872 | tf_op jit(solution)/shard_map/ppermute | solution.py:212
  13.3 23.6 %collective-permute-start.2 = (bf16[256,1024]{1,0:T(8,128)(2,1)S(1)}, bf16[256,1024]{1,0:T(8,128)(2,1)}, u32[]{:S(2)}, u32[]{:S(2)}) collective-permute-start(bf16[256,1024]{1,0:T(8,128)(2,1)S(1)} %get-tuple-element.50), channel_id=1, source_target_pairs={{0,2},{1,3},{2,0},{3,1},{4,6},{5,7},{6,4},{7,5},{8,10},{9,11},{10,... | collective-permute-start | bytes 1572872 | tf_op jit(solution)/shard_map/ppermute | solution.py:212
  14.9 40.3 %collective-permute-start = (bf16[512,1024]{1,0:T(8,128)(2,1)S(1)}, bf16[512,1024]{1,0:T(8,128)(2,1)S(1)}, u32[]{:S(2)}, u32[]{:S(2)}) collective-permute-start(bf16[512,1024]{1,0:T(8,128)(2,1)S(1)} %copy-done), channel_id=1, source_target_pairs={{0,1},{1,0},{2,3},{3,2},{4,5},{5,4},{6,7},{7,6},{8,9},{9,8},{10,11... | collective-permute-start | bytes 3145736 | tf_op jit(solution)/shard_map/ppermute | solution.py:212
  36.8 12.9 %collective-permute-start.3 = (bf16[256,1024]{1,0:T(8,128)(2,1)S(1)}, bf16[256,1024]{1,0:T(8,128)(2,1)}, u32[]{:S(2)}, u32[]{:S(2)}) collective-permute-start(bf16[256,1024]{1,0:T(8,128)(2,1)S(1)} %collective-permute-done.1.refs_4_), channel_id=1, source_target_pairs={{0,2},{1,3},{2,0},{3,1},{4,6},{5,7},{6,4},{7,5},{8,10},{9,11},{10,... | collective-permute-start | bytes 1572872 | tf_op jit(solution)/shard_map/ppermute | solution.py:212
  38.3 15.0 %collective-permute-start.10 = (bf16[256,1024]{1,0:T(8,128)(2,1)}, bf16[256,1024]{1,0:T(8,128)(2,1)}, u32[]{:S(2)}, u32[]{:S(2)}) collective-permute-start(bf16[256,1024]{1,0:T(8,128)(2,1)} %collective-permute-done.2.refs_2_), channel_id=1, source_target_pairs={{0,1},{1,0},{2,3},{3,2},{4,5},{5,4},{6,7},{7,6},{8,9},{9,8},{10,11... | collective-permute-start | bytes 1572872 | tf_op jit(solution)/shard_map/ppermute | solution.py:212
  38.3 16.8 %collective-permute-start.11 = (bf16[256,1024]{1,0:T(8,128)(2,1)S(1)}, bf16[256,1024]{1,0:T(8,128)(2,1)}, u32[]{:S(2)}, u32[]{:S(2)}) collective-permute-start(bf16[256,1024]{1,0:T(8,128)(2,1)S(1)} %collective-permute-done.1.refs_4_), channel_id=1, source_target_pairs={{0,1},{1,0},{2,3},{3,2},{4,5},{5,4},{6,7},{7,6},{8,9},{9,8},{10,11... | collective-permute-start | bytes 1572872 | tf_op jit(solution)/shard_map/ppermute | solution.py:212
  49.7 5.4 %collective-permute-start.12 = (bf16[256,1024]{1,0:T(8,128)(2,1)}, bf16[256,1024]{1,0:T(8,128)(2,1)}, u32[]{:S(2)}, u32[]{:S(2)}) collective-permute-start(bf16[256,1024]{1,0:T(8,128)(2,1)} %collective-permute-done.3.refs_6_), channel_id=1, source_target_pairs={{0,1},{1,0},{2,3},{3,2},{4,5},{5,4},{6,7},{7,6},{8,9},{9,8},{10,11... | collective-permute-start | bytes 1572872 | tf_op jit(solution)/shard_map/ppermute | solution.py:212
  50.3 33.9 %collective-permute-start.6 = (bf16[256,1024]{1,0:T(8,128)(2,1)}, bf16[256,1024]{1,0:T(8,128)(2,1)S(1)}, u32[]{:S(2)}, u32[]{:S(2)}) collective-permute-start(bf16[256,1024]{1,0:T(8,128)(2,1)} %get-tuple-element.27), channel_id=1, source_target_pairs={{0,4},{1,5},{2,6},{3,7},{4,0},{5,1},{6,2},{7,3},{8,12},{9,13},{10,... | collective-permute-start | bytes 1572872 | tf_op jit(solution)/shard_map/ppermute | solution.py:212
  53.4 30.8 %collective-permute-start.4 = (bf16[256,1024]{1,0:T(8,128)(2,1)}, bf16[256,1024]{1,0:T(8,128)(2,1)}, u32[]{:S(2)}, u32[]{:S(2)}) collective-permute-start(bf16[256,1024]{1,0:T(8,128)(2,1)} %get-tuple-element.27), channel_id=1, source_target_pairs={{0,2},{1,3},{2,0},{3,1},{4,6},{5,7},{6,4},{7,5},{8,10},{9,11},{10,... | collective-permute-start | bytes 1572872 | tf_op jit(solution)/shard_map/ppermute | solution.py:212
  84.2 75.8 %all-to-all-start.1 = ((bf16[8,32,3072]{2,1,0:T(8,128)(2,1)}), bf16[8,32,3072]{2,1,0:T(8,128)(2,1)S(1)}, u32[]{:S(2)}, u32[]{:S(2)}) async-start(bf16[8,32,3072]{2,1,0:T(8,128)(2,1)} %bitcast.12), calls=%async_computation.1 | async-start | bytes 3145728 | tf_op jit(solution)/shard_map/all_to_all | solution.py:216
  87.8 39.6 %collective-permute-start.8 = (bf16[256,1024]{1,0:T(8,128)(2,1)S(1)}, bf16[256,1024]{1,0:T(8,128)(2,1)S(1)}, u32[]{:S(2)}, u32[]{:S(2)}) collective-permute-start(bf16[256,1024]{1,0:T(8,128)(2,1)S(1)} %collective-permute-done.6.refs_4_), channel_id=1, source_target_pairs={{0,2},{1,3},{2,0},{3,1},{4,6},{5,7},{6,4},{7,5},{8,10},{9,11},{10,... | collective-permute-start | bytes 1572872 | tf_op jit(solution)/shard_map/ppermute | solution.py:212
  127.5 1.9 collective-permute-start.9
  127.5 3.4 %collective-permute-start.7 = (bf16[256,1024]{1,0:T(8,128)(2,1)S(1)}, bf16[256,1024]{1,0:T(8,128)(2,1)S(1)}, u32[]{:S(2)}, u32[]{:S(2)}) collective-permute-start(bf16[256,1024]{1,0:T(8,128)(2,1)S(1)} %collective-permute-done.6.refs_4_), channel_id=1, source_target_pairs={{0,1},{1,0},{2,3},{3,2},{4,5},{5,4},{6,7},{7,6},{8,9},{9,8},{10,11... | collective-permute-start | bytes 1572872 | tf_op jit(solution)/shard_map/ppermute | solution.py:212
  128.0 3.1 %collective-permute-start.5 = (bf16[256,1024]{1,0:T(8,128)(2,1)}, bf16[256,1024]{1,0:T(8,128)(2,1)S(1)}, u32[]{:S(2)}, u32[]{:S(2)}) collective-permute-start(bf16[256,1024]{1,0:T(8,128)(2,1)} %collective-permute-done.4.refs_2_), channel_id=1, source_target_pairs={{0,1},{1,0},{2,3},{3,2},{4,5},{5,4},{6,7},{7,6},{8,9},{9,8},{10,11... | collective-permute-start | bytes 1572872 | tf_op jit(solution)/shard_map/ppermute | solution.py:212
  160.0 41.6 %all-to-all-start = ((bf16[8,32,3072]{2,1,0:T(8,128)(2,1)}), bf16[8,32,3072]{2,1,0:T(8,128)(2,1)S(1)}, u32[]{:S(2)}, u32[]{:S(2)}) async-start(bf16[8,32,3072]{2,1,0:T(8,128)(2,1)} %bitcast.13), calls=%async_computation | async-start | bytes 3145728 | tf_op jit(solution)/shard_map/all_to_all | solution.py:216
  163.8 15.0 %collective-permute-start.13 = (bf16[256,1024]{1,0:T(8,128)(2,1)}, bf16[256,1024]{1,0:T(8,128)(2,1)}, u32[]{:S(2)}, u32[]{:S(2)}) collective-permute-start(bf16[256,1024]{1,0:T(8,128)(2,1)} %get-tuple-element.33), channel_id=1, source_target_pairs={{0,8},{8,0},{16,24},{24,16},{1,9},{9,1},{17,25},{25,17},{2,10},{10... | collective-permute-start | bytes 1572872 | tf_op jit(solution)/shard_map/ppermute | solution.py:212
  165.4 25.6 %collective-permute-start.14 = (bf16[256,1024]{1,0:T(8,128)(2,1)}, bf16[256,1024]{1,0:T(8,128)(2,1)}, u32[]{:S(2)}, u32[]{:S(2)}) collective-permute-start(bf16[256,1024]{1,0:T(8,128)(2,1)} %get-tuple-element.34), channel_id=1, source_target_pairs={{0,16},{8,24},{16,0},{24,8},{1,17},{9,25},{17,1},{25,9},{2,18},{10... | collective-permute-start | bytes 1572872 | tf_op jit(solution)/shard_map/ppermute | solution.py:212
  166.9 24.1 %collective-permute-start.15 = (bf16[256,1024]{1,0:T(8,128)(2,1)}, bf16[256,1024]{1,0:T(8,128)(2,1)}, u32[]{:S(2)}, u32[]{:S(2)}) collective-permute-start(bf16[256,1024]{1,0:T(8,128)(2,1)} %get-tuple-element.35), channel_id=1, source_target_pairs={{0,24},{8,16},{16,8},{24,0},{1,25},{9,17},{17,9},{25,1},{2,26},{10... | collective-permute-start | bytes 1572872 | tf_op jit(solution)/shard_map/ppermute | solution.py:212
  201.6 42.0 %all-to-all-start.2 = ((bf16[8,32,3072]{2,1,0:T(8,128)(2,1)}), bf16[8,32,3072]{2,1,0:T(8,128)(2,1)S(1)}, u32[]{:S(2)}, u32[]{:S(2)}) async-start(bf16[8,32,3072]{2,1,0:T(8,128)(2,1)} %shard_map.88), calls=%async_computation.2 | async-start | bytes 3145728 | tf_op jit(solution)/shard_map/all_to_all | solution.py:216
  206.6 22.3 %collective-permute-start.16 = (bf16[256,1024]{1,0:T(8,128)(2,1)}, bf16[256,1024]{1,0:T(8,128)(2,1)}, u32[]{:S(2)}, u32[]{:S(2)}) collective-permute-start(bf16[256,1024]{1,0:T(8,128)(2,1)} %get-tuple-element.39.refs_0_), channel_id=1, source_target_pairs={{0,1},{1,0},{2,3},{3,2},{4,5},{5,4},{6,7},{7,6},{8,9},{9,8},{10,11... | collective-permute-start | bytes 1572872 | tf_op jit(solution)/shard_map/ppermute | solution.py:212
  206.8 22.7 %collective-permute-start.17 = (bf16[256,1024]{1,0:T(8,128)(2,1)}, bf16[256,1024]{1,0:T(8,128)(2,1)}, u32[]{:S(2)}, u32[]{:S(2)}) collective-permute-start(bf16[256,1024]{1,0:T(8,128)(2,1)} %collective-permute-done.13.refs_1_), channel_id=1, source_target_pairs={{0,1},{1,0},{2,3},{3,2},{4,5},{5,4},{6,7},{7,6},{8,9},{9,8},{10,11... | collective-permute-start | bytes 1572872 | tf_op jit(solution)/shard_map/ppermute | solution.py:212
  207.1 22.8 %collective-permute-start.18 = (bf16[256,1024]{1,0:T(8,128)(2,1)}, bf16[256,1024]{1,0:T(8,128)(2,1)}, u32[]{:S(2)}, u32[]{:S(2)}) collective-permute-start(bf16[256,1024]{1,0:T(8,128)(2,1)} %collective-permute-done.14.refs_2_), channel_id=1, source_target_pairs={{0,1},{1,0},{2,3},{3,2},{4,5},{5,4},{6,7},{7,6},{8,9},{9,8},{10,11... | collective-permute-start | bytes 1572872 | tf_op jit(solution)/shard_map/ppermute | solution.py:212
  207.3 22.6 %collective-permute-start.19 = (bf16[256,1024]{1,0:T(8,128)(2,1)}, bf16[256,1024]{1,0:T(8,128)(2,1)}, u32[]{:S(2)}, u32[]{:S(2)}) collective-permute-start(bf16[256,1024]{1,0:T(8,128)(2,1)} %collective-permute-done.15.refs_3_), channel_id=1, source_target_pairs={{0,1},{1,0},{2,3},{3,2},{4,5},{5,4},{6,7},{7,6},{8,9},{9,8},{10,11... | collective-permute-start | bytes 1572872 | tf_op jit(solution)/shard_map/ppermute | solution.py:212
  207.6 34.9 %collective-permute-start.22 = (bf16[256,1024]{1,0:T(8,128)(2,1)}, bf16[256,1024]{1,0:T(8,128)(2,1)}, u32[]{:S(2)}, u32[]{:S(2)}) collective-permute-start(bf16[256,1024]{1,0:T(8,128)(2,1)} %get-tuple-element.47), channel_id=1, source_target_pairs={{0,24},{8,16},{16,8},{24,0},{1,25},{9,17},{17,9},{25,1},{2,26},{10... | collective-permute-start | bytes 1572872 | tf_op jit(solution)/shard_map/ppermute | solution.py:212
  229.0 13.8 %collective-permute-start.21 = (bf16[256,1024]{1,0:T(8,128)(2,1)S(1)}, bf16[256,1024]{1,0:T(8,128)(2,1)S(1)}, u32[]{:S(2)}, u32[]{:S(2)}) collective-permute-start(bf16[256,1024]{1,0:T(8,128)(2,1)S(1)} %copy-done.18), channel_id=1, source_target_pairs={{0,16},{8,24},{16,0},{24,8},{1,17},{9,25},{17,1},{25,9},{2,18},{10... | collective-permute-start | bytes 1572872 | tf_op jit(solution)/shard_map/ppermute | solution.py:212
  229.5 14.0 %collective-permute-start.20 = (bf16[256,1024]{1,0:T(8,128)(2,1)S(1)}, bf16[256,1024]{1,0:T(8,128)(2,1)}, u32[]{:S(2)}, u32[]{:S(2)}) collective-permute-start(bf16[256,1024]{1,0:T(8,128)(2,1)S(1)} %copy-done.17), channel_id=1, source_target_pairs={{0,8},{8,0},{16,24},{24,16},{1,9},{9,1},{17,25},{25,17},{2,10},{10... | collective-permute-start | bytes 1572872 | tf_op jit(solution)/shard_map/ppermute | solution.py:212
  243.6 42.6 %all-to-all-start.3 = ((bf16[8,32,3072]{2,1,0:T(8,128)(2,1)}), bf16[8,32,3072]{2,1,0:T(8,128)(2,1)S(1)}, u32[]{:S(2)}, u32[]{:S(2)}) async-start(bf16[8,32,3072]{2,1,0:T(8,128)(2,1)} %shard_map.89), calls=%async_computation.3 | async-start | bytes 3145728 | tf_op jit(solution)/shard_map/all_to_all | solution.py:216
  248.4 18.7 %collective-permute-start.23 = (bf16[256,1024]{1,0:T(8,128)(2,1)}, bf16[256,1024]{1,0:T(8,128)(2,1)S(1)}, u32[]{:S(2)}, u32[]{:S(2)}) collective-permute-start(bf16[256,1024]{1,0:T(8,128)(2,1)} %get-tuple-element.49.refs_0_), channel_id=1, source_target_pairs={{0,1},{1,0},{2,3},{3,2},{4,5},{5,4},{6,7},{7,6},{8,9},{9,8},{10,11... | collective-permute-start | bytes 1572872 | tf_op jit(solution)/shard_map/ppermute | solution.py:212
  248.9 18.2 %collective-permute-start.26 = (bf16[256,1024]{1,0:T(8,128)(2,1)}, bf16[256,1024]{1,0:T(8,128)(2,1)S(1)}, u32[]{:S(2)}, u32[]{:S(2)}) collective-permute-start(bf16[256,1024]{1,0:T(8,128)(2,1)} %collective-permute-done.22.refs_3_), channel_id=1, source_target_pairs={{0,1},{1,0},{2,3},{3,2},{4,5},{5,4},{6,7},{7,6},{8,9},{9,8},{10,11... | collective-permute-start | bytes 1572872 | tf_op jit(solution)/shard_map/ppermute | solution.py:212
  248.9 18.2 %collective-permute-start.25 = (bf16[256,1024]{1,0:T(8,128)(2,1)}, bf16[256,1024]{1,0:T(8,128)(2,1)S(1)}, u32[]{:S(2)}, u32[]{:S(2)}) collective-permute-start(bf16[256,1024]{1,0:T(8,128)(2,1)} %copy-done.8), channel_id=1, source_target_pairs={{0,1},{1,0},{2,3},{3,2},{4,5},{5,4},{6,7},{7,6},{8,9},{9,8},{10,11... | collective-permute-start | bytes 1572872 | tf_op jit(solution)/shard_map/ppermute | solution.py:212
  249.4 17.8 %collective-permute-start.24 = (bf16[256,1024]{1,0:T(8,128)(2,1)}, bf16[256,1024]{1,0:T(8,128)(2,1)S(1)}, u32[]{:S(2)}, u32[]{:S(2)}) collective-permute-start(bf16[256,1024]{1,0:T(8,128)(2,1)} %collective-permute-done.20.refs_1_), channel_id=1, source_target_pairs={{0,1},{1,0},{2,3},{3,2},{4,5},{5,4},{6,7},{7,6},{8,9},{9,8},{10,11... | collective-permute-start | bytes 1572872 | tf_op jit(solution)/shard_map/ppermute | solution.py:212
  (19 other events, 151.9 us)
Sparse Core Ops, SparseCore 0:
  9.8 125.2 all-gather.1

commit v3 on v1

--- a/solution.py
+++ b/solution.py
@@ -136,7 +136,7 @@
 def rotate(piece, rot, chunk, chunks, so_far):
     rows, units = piece.shape
     block = rot.shape[1]
-    tile = 8 * block
+    tile = 4 * block
     held = [] if so_far is None else [so_far]
     return pl.pallas_call(
         rotate_kernel,

time: 279 us -> 280 us (level)
  no operation moved by 1% of the time
where the time goes in v3:
time: 280 us; the launch traced here: 279 us
  Pallas kernels  130 us (46%)
  waiting for transfers between devices  85.6 us (31%)
  starting transfers between devices  38 us (14%)
  between operations  14.2 us (5%)
  local copies, waits for them, and re-layouts  8.76 us (3%)
    ppermute x27, waiting for transfers between devices, swap(): return lax.ppermute(values, axis, [(t, t ^ bits) for t in range(size)])  72.1 us
    pallas_call x2, Pallas kernels, project(): pl.pallas_call(functools.partial(project_kernel, devices, groups, tile, c...  55 us
    pallas_call x4, Pallas kernels, weight_rows(): pl.pallas_call(kernel, grid_spec=pltpu.PrefetchScalarGridSpec(num_scalar_...  52.7 us
    ppermute x27, starting transfers between devices, swap(): return lax.ppermute(values, axis, [(t, t ^ bits) for t in range(size)])  21.7 us
    all_to_all x4, starting transfers between devices, exchange(): return lax.all_to_all(values, axis, split_axis=0, concat_axis=0, tiled=True)  16.3 us
    all_to_all x4, waiting for transfers between devices, exchange(): return lax.all_to_all(values, axis, split_axis=0, concat_axis=0, tiled=True)  12.8 us
    pallas_call x2, Pallas kernels, reorder(): pl.pallas_call(functools.partial(reorder_kernel, block), grid_spec=pltpu....  12 us
    pallas_call x2, Pallas kernels, rotate(): pl.pallas_call(rotate_kernel, grid=(units // tile,), in_specs=[pl.BlockSp...  10.4 us
  transfers between devices with their start and end apart: 32, of which 13 were waited for; matrix products, arithmetic and copies ran while one was open for 1% of the time, Pallas kernels for 45%

profile of v3, /device:TPU:0, one launch (start us, length us, event | category | flops | bytes accessed | tf_op | source)
XLA Modules:
  0.0 278.6 jit_solution(12306287007224042090)
XLA Ops:
  9.3 4.0 %collective-permute-start.1 = (bf16[256,1024]{1,0:T(8,128)(2,1)S(1)}, bf16[256,1024]{1,0:T(8,128)(2,1)S(1)}, u32[]{:S(2)}, u32[]{:S(2)}) collective-permute-start(bf16[256,1024]{1,0:T(8,128)(2,1)S(1)} %get-tuple-element.54), channel_id=1, source_target_pairs={{0,4},{1,5},{2,6},{3,7},{4,0},{5,1},{6,2},{7,3},{8,12},{9,13},{10,... | collective-permute-start | bytes 1572872 | tf_op jit(solution)/shard_map/ppermute | solution.py:212
  13.3 1.6 collective-permute-start.2
  14.9 21.7 %collective-permute-done.1.refs_4_ = bf16[256,1024]{1,0:T(8,128)(2,1)S(1)} collective-permute-done((bf16[256,1024]{1,0:T(8,128)(2,1)S(1)}, bf16[256,1024]{1,0:T(8,128)(2,1)S(1)}, u32[]{:S(2)}, u32[]{:S(2)}) %collective-permute-start.1) | collective-permute-done | bytes 524320 | tf_op jit(solution)/shard_map/ppermute | solution.py:212
  36.8 1.5 collective-permute-start.4
  38.3 2.2 collective-permute-start.3
  40.6 18.8 %collective-permute-done.4.refs_6_ = bf16[256,1024]{1,0:T(8,128)(2,1)} collective-permute-done((bf16[256,1024]{1,0:T(8,128)(2,1)S(1)}, bf16[256,1024]{1,0:T(8,128)(2,1)}, u32[]{:S(2)}, u32[]{:S(2)}) %collective-permute-start.4) | collective-permute-done | bytes 524320 | tf_op jit(solution)/shard_map/ppermute | solution.py:212
  60.4 4.6 %collective-permute-done.3.refs_4_ = bf16[256,1024]{1,0:T(8,128)(2,1)S(1)} collective-permute-done((bf16[256,1024]{1,0:T(8,128)(2,1)}, bf16[256,1024]{1,0:T(8,128)(2,1)S(1)}, u32[]{:S(2)}, u32[]{:S(2)}) %collective-permute-start.3) | collective-permute-done | bytes 524320 | tf_op jit(solution)/shard_map/ppermute | solution.py:212
  65.1 2.0 collective-permute-start.8
  68.1 27.5 %shard_map.86 = (bf16[256,3072]{1,0:T(8,128)(2,1)}, bf16[256,1024]{1,0:T(8,128)(2,1)}, bf16[256,1024]{1,0:T(8,128)(2,1)}, bf16[256,1024]{1,0:T(8,128)(2,1)}, bf16[256,1024]{1,0:T(8,128)(2,1)}) custom-call(s32[2]{0:T(128)} %pad_add_fusion.place_ref, bf16[512,1024]{1,0:T(8,128)(2,1)} %refs_0_.3, bf16[512,1024]{1,0:T(8,128)(2,1)} %copy-done.5, ...), custom_call_target="tpu_custom_call" | custom-call | flops 12884901888 | bytes 60817408 | tf_op jit(solution)/shard_map/pallas_call | solution.py:74
  97.3 4.1 %all-to-all-start.1 = ((bf16[8,32,3072]{2,1,0:T(8,128)(2,1)}), bf16[8,32,3072]{2,1,0:T(8,128)(2,1)S(1)}, u32[]{:S(2)}, u32[]{:S(2)}) async-start(bf16[8,32,3072]{2,1,0:T(8,128)(2,1)} %bitcast.12), calls=%async_computation.1 | async-start | bytes 3145728 | tf_op jit(solution)/shard_map/all_to_all | solution.py:216
  102.4 1.2 collective-permute-done.9.refs_7_
  105.9 27.5 %shard_map.87 = (bf16[256,3072]{1,0:T(8,128)(2,1)}, bf16[256,1024]{1,0:T(8,128)(2,1)}, bf16[256,1024]{1,0:T(8,128)(2,1)}, bf16[256,1024]{1,0:T(8,128)(2,1)}, bf16[256,1024]{1,0:T(8,128)(2,1)}) custom-call(s32[2]{0:T(128)} %pad_add_fusion.place_ref, bf16[512,1024]{1,0:T(8,128)(2,1)} %refs_0_.3, bf16[512,1024]{1,0:T(8,128)(2,1)} %copy-done.5, ...), custom_call_target="tpu_custom_call" | custom-call | flops 12884901888 | bytes 60817408 | tf_op jit(solution)/shard_map/pallas_call | solution.py:74
  133.4 5.8 %all-to-all-done.1.in_ref = bf16[8,32,3072]{2,1,0:T(8,128)(2,1)S(1)} async-done(((bf16[8,32,3072]{2,1,0:T(8,128)(2,1)}), bf16[8,32,3072]{2,1,0:T(8,128)(2,1)S(1)}, u32[]{:S(2)}, u32[]{:S(2)}) %all-to-all-start.1) | async-done | bytes 1572896 | tf_op jit(solution)/shard_map/all_to_all | solution.py:216
  139.2 3.6 %all-to-all-start = ((bf16[8,32,3072]{2,1,0:T(8,128)(2,1)}), bf16[8,32,3072]{2,1,0:T(8,128)(2,1)S(1)}, u32[]{:S(2)}, u32[]{:S(2)}) async-start(bf16[8,32,3072]{2,1,0:T(8,128)(2,1)} %bitcast.13), calls=%async_computation | async-start | bytes 3145728 | tf_op jit(solution)/shard_map/all_to_all | solution.py:216
  142.8 1.5 collective-permute-start.13
  144.3 1.5 collective-permute-start.14
  146.3 11.6 %collective-permute-done.13.refs_1_ = bf16[256,1024]{1,0:T(8,128)(2,1)} collective-permute-done((bf16[256,1024]{1,0:T(8,128)(2,1)}, bf16[256,1024]{1,0:T(8,128)(2,1)}, u32[]{:S(2)}, u32[]{:S(2)}) %collective-permute-start.13) | collective-permute-done | bytes 524320 | tf_op jit(solution)/shard_map/ppermute | solution.py:212
  157.9 11.9 %collective-permute-done.14.refs_2_ = bf16[256,1024]{1,0:T(8,128)(2,1)} collective-permute-done((bf16[256,1024]{1,0:T(8,128)(2,1)}, bf16[256,1024]{1,0:T(8,128)(2,1)}, u32[]{:S(2)}, u32[]{:S(2)}) %collective-permute-start.14) | collective-permute-done | bytes 524320 | tf_op jit(solution)/shard_map/ppermute | solution.py:212
  169.8 6.0 %shard_map.88 = bf16[8,32,3072]{2,1,0:T(8,128)(2,1)} custom-call(s32[192]{0:T(256)} %order_ref.3, bf16[8,32,3072]{2,1,0:T(8,128)(2,1)} %copy-done.2), custom_call_target="tpu_custom_call" | custom-call | bytes 3145728 | tf_op jit(solution)/shard_map/pallas_call | solution.py:112
  175.8 4.8 %all-to-all-done.in_ref = bf16[8,32,3072]{2,1,0:T(8,128)(2,1)S(1)} async-done(((bf16[8,32,3072]{2,1,0:T(8,128)(2,1)}), bf16[8,32,3072]{2,1,0:T(8,128)(2,1)S(1)}, u32[]{:S(2)}, u32[]{:S(2)}) %all-to-all-start) | async-done | bytes 1572896 | tf_op jit(solution)/shard_map/all_to_all | solution.py:216
  180.5 3.8 %all-to-all-start.2 = ((bf16[8,32,3072]{2,1,0:T(8,128)(2,1)}), bf16[8,32,3072]{2,1,0:T(8,128)(2,1)S(1)}, u32[]{:S(2)}, u32[]{:S(2)}) async-start(bf16[8,32,3072]{2,1,0:T(8,128)(2,1)} %shard_map.88), calls=%async_computation.2 | async-start | bytes 3145728 | tf_op jit(solution)/shard_map/all_to_all | solution.py:216
  185.8 2.4 collective-permute-start.22
  188.7 6.0 %shard_map.89 = bf16[8,32,3072]{2,1,0:T(8,128)(2,1)} custom-call(s32[192]{0:T(256)} %order_ref.3, bf16[8,32,3072]{2,1,0:T(8,128)(2,1)} %copy-done.1), custom_call_target="tpu_custom_call" | custom-call | bytes 3145728 | tf_op jit(solution)/shard_map/pallas_call | solution.py:112
  194.7 12.7 %shard_map.90.refs_5_ = bf16[2048,3072]{1,0:T(8,128)(2,1)} custom-call(s32[2]{0:T(128)} %pad_add_fusion.2.place_ref, bf16[256,1024]{1,0:T(8,128)(2,1)} %get-tuple-element.43.refs_0_, bf16[256,1024]{1,0:T(8,128)(2,1)} %collective-permute-done.13.refs_1_, bf16[256,1024]{1,0:T(8,128)(2,1)} %collective-permute-done.14.refs_2_, ...), custom_call_target="tpu_custom_call" | custom-call | flops 6442450944 | bytes 20971520 | tf_op jit(solution)/shard_map/pallas_call | solution.py:188
  208.6 12.6 %shard_map.91.refs_5_ = bf16[2048,3072]{1,0:T(8,128)(2,1)} custom-call(s32[2]{0:T(128)} %pad_add_fusion.1.place_ref, bf16[256,1024]{1,0:T(8,128)(2,1)} %collective-permute-done.16.refs_0_, bf16[256,1024]{1,0:T(8,128)(2,1)} %collective-permute-done.17.refs_1_, bf16[256,1024]{1,0:T(8,128)(2,1)} %collective-permute-done.18.refs_2_, ...), custom_call_target="tpu_custom_call", output_to_operand_aliasing={{}: (6, {})} | custom-call | flops 6442450944 | bytes 20971520 | tf_op jit(solution)/shard_map/pallas_call | solution.py:188
  222.7 4.8 %all-to-all-start.3 = ((bf16[8,32,3072]{2,1,0:T(8,128)(2,1)}), bf16[8,32,3072]{2,1,0:T(8,128)(2,1)S(1)}, u32[]{:S(2)}, u32[]{:S(2)}) async-start(bf16[8,32,3072]{2,1,0:T(8,128)(2,1)} %shard_map.89), calls=%async_computation.3 | async-start | bytes 3145728 | tf_op jit(solution)/shard_map/all_to_all | solution.py:216
  228.5 5.2 %shard_map.92.refs_0_ = bf16[512,3072]{1,0:T(8,128)(2,1)} custom-call(bf16[256,3072]{1,0:T(8,128)(2,1)} %bitcast.9, bf16[24,128,128]{2,1,0:T(8,128)(2,1)} %rot_ref.3), custom_call_target="tpu_custom_call" | custom-call | flops 201326592 | bytes 3145728 | tf_op jit(solution)/shard_map/pallas_call | solution.py:141
  233.7 13.7 %shard_map.94.refs_5_ = bf16[2048,3072]{1,0:T(8,128)(2,1)} custom-call(s32[2]{0:T(128)} %pad_add_fusion.2.place_ref, bf16[256,1024]{1,0:T(8,128)(2,1)} %get-tuple-element.53.refs_0_, bf16[256,1024]{1,0:T(8,128)(2,1)} %collective-permute-done.20.refs_1_, bf16[256,1024]{1,0:T(8,128)(2,1)} %copy-done.8, ...), custom_call_target="tpu_custom_call", output_to_operand_aliasing={{}: (6, {})} | custom-call | flops 6442450944 | bytes 20971520 | tf_op jit(solution)/shard_map/pallas_call | solution.py:188
  249.4 13.7 %shard_map.95 = bf16[2048,3072]{1,0:T(8,128)(2,1)} custom-call(s32[2]{0:T(128)} %pad_add_fusion.1.place_ref, bf16[256,1024]{1,0:T(8,128)(2,1)} %copy-done.13, bf16[256,1024]{1,0:T(8,128)(2,1)} %copy-done.17, bf16[256,1024]{1,0:T(8,128)(2,1)} %copy-done.15, bf16[256,1024]{1,0:T(8,128)(2,1)} %copy-done.14, ...), custom_call_target="tpu_custom_call", output_to_operand_aliasing={{}: (6, {})} | custom-call | flops 6442450944 | bytes 20971520 | tf_op jit(solution)/shard_map/pallas_call | solution.py:188
  263.1 2.2 all-to-all-done.3
  265.3 1.2 copy-done.4
  266.5 5.2 %shard_map.93 = bf16[512,3072]{1,0:T(8,128)(2,1)} custom-call(bf16[256,3072]{1,0:T(8,128)(2,1)} %bitcast.10, bf16[24,128,128]{2,1,0:T(8,128)(2,1)} %rot_ref.3, bf16[512,3072]{1,0:T(8,128)(2,1)} %shard_map.92.refs_0_), custom_call_target="tpu_custom_call", output_to_operand_aliasing={{}: (2, {})} | custom-call | flops 201326592 | bytes 3145728 | tf_op jit(solution)/shard_map/pallas_call | solution.py:141
  (91 shorter events, 17.5 us)
Async XLA Ops:
  7.2 187.5 %all-gather.2.cloned.1.call-start = ((), (), s32[]{:S(2)}) async-start(), calls=%async_computation.4 | async-start | bytes 15728640 | tf_op jit(solution)/shard_map/all_gather | solution.py:232
  9.3 27.3 %collective-permute-start.1 = (bf16[256,1024]{1,0:T(8,128)(2,1)S(1)}, bf16[256,1024]{1,0:T(8,128)(2,1)S(1)}, u32[]{:S(2)}, u32[]{:S(2)}) collective-permute-start(bf16[256,1024]{1,0:T(8,128)(2,1)S(1)} %get-tuple-element.54), channel_id=1, source_target_pairs={{0,4},{1,5},{2,6},{3,7},{4,0},{5,1},{6,2},{7,3},{8,12},{9,13},{10,... | collective-permute-start | bytes 1572872 | tf_op jit(solution)/shard_map/ppermute | solution.py:212
  13.3 23.6 %collective-permute-start.2 = (bf16[256,1024]{1,0:T(8,128)(2,1)S(1)}, bf16[256,1024]{1,0:T(8,128)(2,1)}, u32[]{:S(2)}, u32[]{:S(2)}) collective-permute-start(bf16[256,1024]{1,0:T(8,128)(2,1)S(1)} %get-tuple-element.54), channel_id=1, source_target_pairs={{0,2},{1,3},{2,0},{3,1},{4,6},{5,7},{6,4},{7,5},{8,10},{9,11},{10,... | collective-permute-start | bytes 1572872 | tf_op jit(solution)/shard_map/ppermute | solution.py:212
  36.8 22.5 %collective-permute-start.4 = (bf16[256,1024]{1,0:T(8,128)(2,1)S(1)}, bf16[256,1024]{1,0:T(8,128)(2,1)}, u32[]{:S(2)}, u32[]{:S(2)}) collective-permute-start(bf16[256,1024]{1,0:T(8,128)(2,1)S(1)} %collective-permute-done.1.refs_4_), channel_id=1, source_target_pairs={{0,2},{1,3},{2,0},{3,1},{4,6},{5,7},{6,4},{7,5},{8,10},{9,11},{10,... | collective-permute-start | bytes 1572872 | tf_op jit(solution)/shard_map/ppermute | solution.py:212
  38.3 28.8 %collective-permute-start = (bf16[512,1024]{1,0:T(8,128)(2,1)S(1)}, bf16[512,1024]{1,0:T(8,128)(2,1)S(1)}, u32[]{:S(2)}, u32[]{:S(2)}) collective-permute-start(bf16[512,1024]{1,0:T(8,128)(2,1)S(1)} %copy-done), channel_id=1, source_target_pairs={{0,1},{1,0},{2,3},{3,2},{4,5},{5,4},{6,7},{7,6},{8,9},{9,8},{10,11... | collective-permute-start | bytes 3145736 | tf_op jit(solution)/shard_map/ppermute | solution.py:212
  38.3 26.7 %collective-permute-start.3 = (bf16[256,1024]{1,0:T(8,128)(2,1)}, bf16[256,1024]{1,0:T(8,128)(2,1)S(1)}, u32[]{:S(2)}, u32[]{:S(2)}) collective-permute-start(bf16[256,1024]{1,0:T(8,128)(2,1)} %get-tuple-element.30), channel_id=1, source_target_pairs={{0,4},{1,5},{2,6},{3,7},{4,0},{5,1},{6,2},{7,3},{8,12},{9,13},{10,... | collective-permute-start | bytes 1572872 | tf_op jit(solution)/shard_map/ppermute | solution.py:212
  59.3 5.8 %collective-permute-start.12 = (bf16[256,1024]{1,0:T(8,128)(2,1)}, bf16[256,1024]{1,0:T(8,128)(2,1)}, u32[]{:S(2)}, u32[]{:S(2)}) collective-permute-start(bf16[256,1024]{1,0:T(8,128)(2,1)} %collective-permute-done.4.refs_6_), channel_id=1, source_target_pairs={{0,1},{1,0},{2,3},{3,2},{4,5},{5,4},{6,7},{7,6},{8,9},{9,8},{10,11... | collective-permute-start | bytes 1572872 | tf_op jit(solution)/shard_map/ppermute | solution.py:212
  59.3 7.8 %collective-permute-start.10 = (bf16[256,1024]{1,0:T(8,128)(2,1)}, bf16[256,1024]{1,0:T(8,128)(2,1)}, u32[]{:S(2)}, u32[]{:S(2)}) collective-permute-start(bf16[256,1024]{1,0:T(8,128)(2,1)} %collective-permute-done.2.refs_2_), channel_id=1, source_target_pairs={{0,1},{1,0},{2,3},{3,2},{4,5},{5,4},{6,7},{7,6},{8,9},{9,8},{10,11... | collective-permute-start | bytes 1572872 | tf_op jit(solution)/shard_map/ppermute | solution.py:212
  59.8 7.3 %collective-permute-start.11 = (bf16[256,1024]{1,0:T(8,128)(2,1)S(1)}, bf16[256,1024]{1,0:T(8,128)(2,1)}, u32[]{:S(2)}, u32[]{:S(2)}) collective-permute-start(bf16[256,1024]{1,0:T(8,128)(2,1)S(1)} %collective-permute-done.1.refs_4_), channel_id=1, source_target_pairs={{0,1},{1,0},{2,3},{3,2},{4,5},{5,4},{6,7},{7,6},{8,9},{9,8},{10,11... | collective-permute-start | bytes 1572872 | tf_op jit(solution)/shard_map/ppermute | solution.py:212
  65.1 30.6 %collective-permute-start.5 = (bf16[256,1024]{1,0:T(8,128)(2,1)}, bf16[256,1024]{1,0:T(8,128)(2,1)S(1)}, u32[]{:S(2)}, u32[]{:S(2)}) collective-permute-start(bf16[256,1024]{1,0:T(8,128)(2,1)} %get-tuple-element.30), channel_id=1, source_target_pairs={{0,2},{1,3},{2,0},{3,1},{4,6},{5,7},{6,4},{7,5},{8,10},{9,11},{10,... | collective-permute-start | bytes 1572872 | tf_op jit(solution)/shard_map/ppermute | solution.py:212
  65.1 30.6 %collective-permute-start.8 = (bf16[256,1024]{1,0:T(8,128)(2,1)S(1)}, bf16[256,1024]{1,0:T(8,128)(2,1)S(1)}, u32[]{:S(2)}, u32[]{:S(2)}) collective-permute-start(bf16[256,1024]{1,0:T(8,128)(2,1)S(1)} %collective-permute-done.3.refs_4_), channel_id=1, source_target_pairs={{0,2},{1,3},{2,0},{3,1},{4,6},{5,7},{6,4},{7,5},{8,10},{9,11},{10,... | collective-permute-start | bytes 1572872 | tf_op jit(solution)/shard_map/ppermute | solution.py:212
  97.3 41.9 %all-to-all-start.1 = ((bf16[8,32,3072]{2,1,0:T(8,128)(2,1)}), bf16[8,32,3072]{2,1,0:T(8,128)(2,1)S(1)}, u32[]{:S(2)}, u32[]{:S(2)}) async-start(bf16[8,32,3072]{2,1,0:T(8,128)(2,1)} %bitcast.12), calls=%async_computation.1 | async-start | bytes 3145728 | tf_op jit(solution)/shard_map/all_to_all | solution.py:216
  101.4 2.2 collective-permute-start.9
  101.9 2.4 collective-permute-start.7
  102.0 3.1 %collective-permute-start.6 = (bf16[256,1024]{1,0:T(8,128)(2,1)S(1)}, bf16[256,1024]{1,0:T(8,128)(2,1)S(1)}, u32[]{:S(2)}, u32[]{:S(2)}) collective-permute-start(bf16[256,1024]{1,0:T(8,128)(2,1)S(1)} %copy-done.10), channel_id=1, source_target_pairs={{0,1},{1,0},{2,3},{3,2},{4,5},{5,4},{6,7},{7,6},{8,9},{9,8},{10,11... | collective-permute-start | bytes 1572872 | tf_op jit(solution)/shard_map/ppermute | solution.py:212
  139.2 41.3 %all-to-all-start = ((bf16[8,32,3072]{2,1,0:T(8,128)(2,1)}), bf16[8,32,3072]{2,1,0:T(8,128)(2,1)S(1)}, u32[]{:S(2)}, u32[]{:S(2)}) async-start(bf16[8,32,3072]{2,1,0:T(8,128)(2,1)} %bitcast.13), calls=%async_computation | async-start | bytes 3145728 | tf_op jit(solution)/shard_map/all_to_all | solution.py:216
  142.8 15.1 %collective-permute-start.13 = (bf16[256,1024]{1,0:T(8,128)(2,1)}, bf16[256,1024]{1,0:T(8,128)(2,1)}, u32[]{:S(2)}, u32[]{:S(2)}) collective-permute-start(bf16[256,1024]{1,0:T(8,128)(2,1)} %get-tuple-element.37), channel_id=1, source_target_pairs={{0,8},{8,0},{16,24},{24,16},{1,9},{9,1},{17,25},{25,17},{2,10},{10... | collective-permute-start | bytes 1572872 | tf_op jit(solution)/shard_map/ppermute | solution.py:212
  144.3 25.4 %collective-permute-start.14 = (bf16[256,1024]{1,0:T(8,128)(2,1)}, bf16[256,1024]{1,0:T(8,128)(2,1)}, u32[]{:S(2)}, u32[]{:S(2)}) collective-permute-start(bf16[256,1024]{1,0:T(8,128)(2,1)} %get-tuple-element.38), channel_id=1, source_target_pairs={{0,16},{8,24},{16,0},{24,8},{1,17},{9,25},{17,1},{25,9},{2,18},{10... | collective-permute-start | bytes 1572872 | tf_op jit(solution)/shard_map/ppermute | solution.py:212
  145.8 23.9 %collective-permute-start.15 = (bf16[256,1024]{1,0:T(8,128)(2,1)}, bf16[256,1024]{1,0:T(8,128)(2,1)}, u32[]{:S(2)}, u32[]{:S(2)}) collective-permute-start(bf16[256,1024]{1,0:T(8,128)(2,1)} %get-tuple-element.39), channel_id=1, source_target_pairs={{0,24},{8,16},{16,8},{24,0},{1,25},{9,17},{17,9},{25,1},{2,26},{10... | collective-permute-start | bytes 1572872 | tf_op jit(solution)/shard_map/ppermute | solution.py:212
  180.5 42.1 %all-to-all-start.2 = ((bf16[8,32,3072]{2,1,0:T(8,128)(2,1)}), bf16[8,32,3072]{2,1,0:T(8,128)(2,1)S(1)}, u32[]{:S(2)}, u32[]{:S(2)}) async-start(bf16[8,32,3072]{2,1,0:T(8,128)(2,1)} %shard_map.88), calls=%async_computation.2 | async-start | bytes 3145728 | tf_op jit(solution)/shard_map/all_to_all | solution.py:216
  185.6 21.9 %collective-permute-start.16 = (bf16[256,1024]{1,0:T(8,128)(2,1)}, bf16[256,1024]{1,0:T(8,128)(2,1)}, u32[]{:S(2)}, u32[]{:S(2)}) collective-permute-start(bf16[256,1024]{1,0:T(8,128)(2,1)} %get-tuple-element.43.refs_0_), channel_id=1, source_target_pairs={{0,1},{1,0},{2,3},{3,2},{4,5},{5,4},{6,7},{7,6},{8,9},{9,8},{10,11... | collective-permute-start | bytes 1572872 | tf_op jit(solution)/shard_map/ppermute | solution.py:212
  185.8 35.4 %collective-permute-start.22 = (bf16[256,1024]{1,0:T(8,128)(2,1)}, bf16[256,1024]{1,0:T(8,128)(2,1)}, u32[]{:S(2)}, u32[]{:S(2)}) collective-permute-start(bf16[256,1024]{1,0:T(8,128)(2,1)} %get-tuple-element.51), channel_id=1, source_target_pairs={{0,24},{8,16},{16,8},{24,0},{1,25},{9,17},{17,9},{25,1},{2,26},{10... | collective-permute-start | bytes 1572872 | tf_op jit(solution)/shard_map/ppermute | solution.py:212
  188.2 19.9 %collective-permute-start.17 = (bf16[256,1024]{1,0:T(8,128)(2,1)}, bf16[256,1024]{1,0:T(8,128)(2,1)}, u32[]{:S(2)}, u32[]{:S(2)}) collective-permute-start(bf16[256,1024]{1,0:T(8,128)(2,1)} %collective-permute-done.13.refs_1_), channel_id=1, source_target_pairs={{0,1},{1,0},{2,3},{3,2},{4,5},{5,4},{6,7},{7,6},{8,9},{9,8},{10,11... | collective-permute-start | bytes 1572872 | tf_op jit(solution)/shard_map/ppermute | solution.py:212
  188.2 20.4 %collective-permute-start.18 = (bf16[256,1024]{1,0:T(8,128)(2,1)}, bf16[256,1024]{1,0:T(8,128)(2,1)}, u32[]{:S(2)}, u32[]{:S(2)}) collective-permute-start(bf16[256,1024]{1,0:T(8,128)(2,1)} %collective-permute-done.14.refs_2_), channel_id=1, source_target_pairs={{0,1},{1,0},{2,3},{3,2},{4,5},{5,4},{6,7},{7,6},{8,9},{9,8},{10,11... | collective-permute-start | bytes 1572872 | tf_op jit(solution)/shard_map/ppermute | solution.py:212
  188.7 19.9 %collective-permute-start.19 = (bf16[256,1024]{1,0:T(8,128)(2,1)}, bf16[256,1024]{1,0:T(8,128)(2,1)}, u32[]{:S(2)}, u32[]{:S(2)}) collective-permute-start(bf16[256,1024]{1,0:T(8,128)(2,1)} %collective-permute-done.15.refs_3_), channel_id=1, source_target_pairs={{0,1},{1,0},{2,3},{3,2},{4,5},{5,4},{6,7},{7,6},{8,9},{9,8},{10,11... | collective-permute-start | bytes 1572872 | tf_op jit(solution)/shard_map/ppermute | solution.py:212
  207.5 14.4 %collective-permute-start.21 = (bf16[256,1024]{1,0:T(8,128)(2,1)S(1)}, bf16[256,1024]{1,0:T(8,128)(2,1)S(1)}, u32[]{:S(2)}, u32[]{:S(2)}) collective-permute-start(bf16[256,1024]{1,0:T(8,128)(2,1)S(1)} %copy-done.21), channel_id=1, source_target_pairs={{0,16},{8,24},{16,0},{24,8},{1,17},{9,25},{17,1},{25,9},{2,18},{10... | collective-permute-start | bytes 1572872 | tf_op jit(solution)/shard_map/ppermute | solution.py:212
  208.0 14.6 %collective-permute-start.20 = (bf16[256,1024]{1,0:T(8,128)(2,1)S(1)}, bf16[256,1024]{1,0:T(8,128)(2,1)}, u32[]{:S(2)}, u32[]{:S(2)}) collective-permute-start(bf16[256,1024]{1,0:T(8,128)(2,1)S(1)} %copy-done.20), channel_id=1, source_target_pairs={{0,8},{8,0},{16,24},{24,16},{1,9},{9,1},{17,25},{25,17},{2,10},{10... | collective-permute-start | bytes 1572872 | tf_op jit(solution)/shard_map/ppermute | solution.py:212
  222.7 42.6 %all-to-all-start.3 = ((bf16[8,32,3072]{2,1,0:T(8,128)(2,1)}), bf16[8,32,3072]{2,1,0:T(8,128)(2,1)S(1)}, u32[]{:S(2)}, u32[]{:S(2)}) async-start(bf16[8,32,3072]{2,1,0:T(8,128)(2,1)} %shard_map.89), calls=%async_computation.3 | async-start | bytes 3145728 | tf_op jit(solution)/shard_map/all_to_all | solution.py:216
  227.5 19.9 %collective-permute-start.23 = (bf16[256,1024]{1,0:T(8,128)(2,1)}, bf16[256,1024]{1,0:T(8,128)(2,1)S(1)}, u32[]{:S(2)}, u32[]{:S(2)}) collective-permute-start(bf16[256,1024]{1,0:T(8,128)(2,1)} %get-tuple-element.53.refs_0_), channel_id=1, source_target_pairs={{0,1},{1,0},{2,3},{3,2},{4,5},{5,4},{6,7},{7,6},{8,9},{9,8},{10,11... | collective-permute-start | bytes 1572872 | tf_op jit(solution)/shard_map/ppermute | solution.py:212
  228.0 19.4 %collective-permute-start.26 = (bf16[256,1024]{1,0:T(8,128)(2,1)}, bf16[256,1024]{1,0:T(8,128)(2,1)S(1)}, u32[]{:S(2)}, u32[]{:S(2)}) collective-permute-start(bf16[256,1024]{1,0:T(8,128)(2,1)} %collective-permute-done.22.refs_3_), channel_id=1, source_target_pairs={{0,1},{1,0},{2,3},{3,2},{4,5},{5,4},{6,7},{7,6},{8,9},{9,8},{10,11... | collective-permute-start | bytes 1572872 | tf_op jit(solution)/shard_map/ppermute | solution.py:212
  228.0 19.5 %collective-permute-start.25 = (bf16[256,1024]{1,0:T(8,128)(2,1)}, bf16[256,1024]{1,0:T(8,128)(2,1)S(1)}, u32[]{:S(2)}, u32[]{:S(2)}) collective-permute-start(bf16[256,1024]{1,0:T(8,128)(2,1)} %copy-done.8), channel_id=1, source_target_pairs={{0,1},{1,0},{2,3},{3,2},{4,5},{5,4},{6,7},{7,6},{8,9},{9,8},{10,11... | collective-permute-start | bytes 1572872 | tf_op jit(solution)/shard_map/ppermute | solution.py:212
  228.5 19.0 %collective-permute-start.24 = (bf16[256,1024]{1,0:T(8,128)(2,1)}, bf16[256,1024]{1,0:T(8,128)(2,1)S(1)}, u32[]{:S(2)}, u32[]{:S(2)}) collective-permute-start(bf16[256,1024]{1,0:T(8,128)(2,1)} %collective-permute-done.20.refs_1_), channel_id=1, source_target_pairs={{0,1},{1,0},{2,3},{3,2},{4,5},{5,4},{6,7},{7,6},{8,9},{9,8},{10,11... | collective-permute-start | bytes 1572872 | tf_op jit(solution)/shard_map/ppermute | solution.py:212
  (22 other events, 159.5 us)
Sparse Core Ops, SparseCore 0:
  9.8 125.2 all-gather.1
